TPU v7x, 32 devices: a whole 2x2x4 slice. The times are simulated.
32 devices in a mesh: dp: 16 (over z, y, x), seq: 2 (over core).
Axes of the slice: x: 2, y: 2, z: 4, core: 2. Of those that a mesh axis runs over, the one named last changes fastest.
Arguments:
- tokens: bfloat16 [64, 512, 768], P('dp', 'seq'), may hold values from -6 to 6
- cotangent: bfloat16 [64, 512, 768], P('dp', 'seq'), may hold values from -6 to 6
- seq_lengths: int32 [16, 4], P('dp'), may hold values from 1 to 512, 1536 in all within a row
- slot_order: int32 [16, 4], P('dp'), may hold values from 0 to 3, each once within a row
- attn_weights: float32 [768, 3072], P(None, ('dp', 'seq'))
- attn_moment: float32 [768, 3072], P(None, ('dp', 'seq'))
- attn_second: float32 [768, 3072], P(None, ('dp', 'seq')), as said below
- ffn_weights: float32 [768, 6144], P(None, ('dp', 'seq'))
- ffn_moment: float32 [768, 6144], P(None, ('dp', 'seq'))
- ffn_second: float32 [768, 6144], P(None, ('dp', 'seq')), as said below
- vectors: float32 [9216], P(('dp', 'seq'))
- vector_moment: float32 [9216], P(('dp', 'seq'))
- vector_second: float32 [9216], P(('dp', 'seq')), as said below
Outputs:
- layer_out: bfloat16 [64, 512, 768], P('dp', 'seq')
- input_grad: float32 [64, 512, 768], P('dp', 'seq')
- attn_moment_out: float32 [768, 3072], P(None, ('dp', 'seq'))
- attn_second_out: float32 [768, 3072], P(None, ('dp', 'seq'))
- attn_weights_out: float32 [768, 3072], P(None, ('dp', 'seq'))
- attn_copy_out: bfloat16 [768, 3072], P(None, ('dp', 'seq'))
- ffn_moment_out: float32 [768, 6144], P(None, ('dp', 'seq'))
- ffn_second_out: float32 [768, 6144], P(None, ('dp', 'seq'))
- ffn_weights_out: float32 [768, 6144], P(None, ('dp', 'seq'))
- ffn_copy_out: bfloat16 [768, 6144], P(None, ('dp', 'seq'))
- vector_moment_out: float32 [9216], P(('dp', 'seq'))
- vector_second_out: float32 [9216], P(('dp', 'seq'))
- vectors_out: float32 [9216], P(('dp', 'seq'))
- vector_copy_out: bfloat16 [9216], P(('dp', 'seq'))
Inputs may be any that keep to these rules, and one draw needn't show every extreme that they name: `seq_lengths`: in each group the 4 lengths sum to 1536 and the largest is exactly 512. `slot_order`: each group's row is a permutation of 0 to 3. `attn_second`: Positive. `ffn_second`: Positive. `vector_second`: Positive.
All inputs are finite; a program needn't handle non-finite values.
Results may differ from a plain program's by a relative error of at most 0.012.
The roundings to bfloat16 on the way count: a program that leaves them out, or rounds other values in their place, can miss the bound.
Values may be sent and summed in bfloat16 or wider, within the bound.
No kernel may reach another device: no remote copies, remote signals or barrier semaphores. Data moves between devices by JAX's collectives and lax.ppermute only.
A program may use at most 192 MiB of HBM per device.

v0:
```python
import math

import jax
import jax.numpy as jnp
from jax import lax
from jax.experimental import pallas as pl
from jax.experimental.pallas import tpu as pltpu
from jax.sharding import PartitionSpec as P

H = 12
FF = 3072
STEP = 5

epsilon = 1e-06
masked_score = -1e30
decay_rate = 0.5
adam_epsilon = 1e-08
weight_decay = 0.01
vector_rate = 0.5

AXES = ("dp", "seq")
BF = jnp.bfloat16
F32 = jnp.float32
VMEM_LIMIT = 56 * 1024 * 1024
TILE = 256
COST = 16
ANY = pl.BlockSpec(memory_space=pl.ANY)
SMEM = pl.BlockSpec(memory_space=pltpu.SMEM)
VMEM = pl.BlockSpec(memory_space=pltpu.VMEM)


def nn(a, b):
    return lax.dot_general(a, b, (((1,), (0,)), ((), ())), preferred_element_type=F32)


def nt(a, b):
    return lax.dot_general(a, b, (((1,), (1,)), ((), ())), preferred_element_type=F32)


def tn(a, b):
    return lax.dot_general(a, b, (((0,), (0,)), ((), ())), preferred_element_type=F32)


class Grid:
    def __init__(self, chips):
        power = chips.bit_length() - 1
        if 1 << power == chips:
            self.side = 1 << (power // 3)
            self.nz = chips // (self.side * self.side)
        else:
            self.side, self.nz = 1, chips
        self.devices = 2 * chips
        self.xor = 1 << power == chips

    def z_mask(self, m):
        return m * 2 * self.side * self.side

    def x_mask(self, m):
        return 2 * m

    def y_mask(self, m):
        return 2 * m * self.side

    def label(self, core, other, i3, i2, iz):
        x = jnp.where(core == 0, i2, i3)
        y = jnp.where(core == 0, i3, i2)
        return self.z_mask(iz) + self.y_mask(y) + self.x_mask(x) + other


def permute(value, grid, mask_of_core):
    pairs = [(i, i ^ mask_of_core(i & 1)) for i in range(grid.devices)]
    return lax.ppermute(value, AXES, pairs)


def along_two(grid, value, m):
    return permute(value, grid, lambda c: grid.x_mask(m) if c == 0 else grid.y_mask(m))


def along_three(grid, value, m):
    return permute(value, grid, lambda c: grid.y_mask(m) if c == 0 else grid.x_mask(m))


def gather_z(grid, block):
    return [block] + [permute(block, grid, lambda c: grid.z_mask(m)) for m in range(1, grid.nz)]


def gather_two(grid, zed):
    return [zed] + [along_two(grid, zed, m) for m in range(1, grid.side)]


def gather_three(grid, two):
    return [along_three(grid, t, m) for m in range(1, grid.side) for t in two]


def with_core(grid, own, deps):
    own = [gate(own[0], deps) if deps else own[0]] + own[1:]
    return own + [permute(p, grid, lambda c: 1) for p in own]


def is_path(grid, rows):
    return grid.side == 2 and grid.nz == 4 and rows % 16 == 0


def slot_of(grid, label, core):
    other = label & 1
    x = (label // 2) & (grid.side - 1)
    y = (label // (2 * grid.side)) & (grid.side - 1)
    z = label // (2 * grid.side * grid.side)
    first = (core ^ other) == 0
    i2 = jnp.where(first, x, y)
    i3 = jnp.where(first, y, x)
    return other, (i3 * grid.side + i2) * grid.nz + z


def natural_vectors(grid, pieces, core, me, row, count):
    side, nz = grid.side, grid.nz
    table = jnp.stack([p[:, row, :count] for p in pieces]).reshape(2, side, side, nz, count)
    turned = jnp.swapaxes(table, 1, 2)
    first = jnp.stack([table[0], turned[1]])
    second = jnp.stack([turned[0], table[1]])
    value = jnp.where(core == 0, first, second)
    value = jnp.transpose(value, (3, 1, 2, 0, 4)).reshape(grid.devices, count)
    bit = 1
    while bit < grid.devices:
        pairs = value.reshape(-1, 2, bit, count)
        value = jnp.where((me & bit) == 0, pairs, pairs[:, ::-1]).reshape(grid.devices, count)
        bit *= 2
    return value.reshape(1, -1).astype(F32)


def start_natural(grid, me_ref, pieces, dest, sems, first=0, last=None, order=None):
    last = grid.devices if last is None else last
    rows = dest.shape[0] // (last - first)
    if len(pieces) == 1:
        pltpu.make_async_copy(
            pieces[0].at[pl.ds(first * rows, (last - first) * rows)], dest, sems.at[0]
        ).start()
        return
    me = me_ref[0]
    core = me & 1
    side, nz = grid.side, grid.nz
    for label in sorted(range(grid.devices), key=order or (lambda j: j // (2 * side * side))):
        other, x, y = label & 1, label // 2 % side, label // (2 * side) % side
        iz = label // (2 * side * side)
        block = me ^ label

        def start(ref, block=block, iz=iz):
            row = pl.multiple_of((block - first) * rows, rows)
            pltpu.make_async_copy(
                ref.at[iz, pl.ds(0, rows)], dest.at[pl.ds(row, rows)], sems.at[block]
            ).start()

        def either(other=other, x=x, y=y, start=start):
            one = pieces[(other * side + y) * side + x]
            two = pieces[(other * side + x) * side + y]
            if x == y:
                start(one)
            else:
                pl.when((core ^ other) == 0)(lambda: start(one))
                pl.when((core ^ other) != 0)(lambda: start(two))

        if last - first == grid.devices:
            either()
        else:
            pl.when((block >= first) & (block < last))(either)


def wait_natural(grid, pieces, dest, sems, begin, count, first=0, last=None):
    last = grid.devices if last is None else last
    rows = dest.shape[0] // (last - first)
    if len(pieces) == 1:

        @pl.when(begin == first)
        def _():
            pltpu.make_async_copy(
                pieces[0].at[pl.ds(first * rows, (last - first) * rows)], dest, sems.at[0]
            ).wait()

        return
    for i in range(count):
        block = begin + i
        pltpu.make_async_copy(
            pieces[0].at[0, pl.ds(0, rows)],
            dest.at[pl.ds(pl.multiple_of((block - first) * rows, rows), rows)],
            sems.at[block],
        ).wait()


def path_shapes(grid, blocks, per, width):
    if not is_path(grid, per):
        return [
            jax.ShapeDtypeStruct((blocks * per, width), BF),
            jax.ShapeDtypeStruct((blocks, 8, width), BF),
        ]
    return [jax.ShapeDtypeStruct((grid.nz, per, width), BF)] * 8


def start_store(core, src, dests, x, y, other, iz, sem):
    one, two = (dests[4 * other + k].at[iz] for k in (2 * y + x, 2 * x + y))
    copy = pltpu.make_async_copy(src, one, sem)
    if x == y:
        copy.start()
    else:
        pl.when((core ^ other) == 0)(lambda: copy.start())
        pl.when((core ^ other) != 0)(lambda: pltpu.make_async_copy(src, two, sem).start())
    return copy


class Sums:
    def __init__(self, grid, path, blocks):
        self.grid, self.path = grid, path
        self.three, self.two, self.z = [], [], []
        if path:
            self.keep = list(blocks[:4])
            got = {k: permute(blocks[4 + k], grid, lambda c: 1) for k in (3, 2, 1, 0)}
            self.core = [got[k] for k in range(4)]
        else:
            self.keep = list(blocks)

    def terms(self, i3, i2, iz):
        grid = self.grid
        at = i3 * grid.side + i2
        total = self.keep[at][iz].astype(F32) + self.core[at][iz].astype(F32)
        if i3 == 0:
            for there, got in self.three:
                if there == i2:
                    total = total + got[iz].astype(F32)
            if i2 == 0:
                for got in self.two:
                    total = total + got[iz].astype(F32)
        return total

    def add_core(self):
        if not self.path:
            return []
        grid = self.grid
        every = slice(0, grid.nz)
        sends = [
            (i2, m, self.terms(m, i2, every).astype(BF))
            for i2 in reversed(range(grid.side))
            for m in range(1, grid.side)
        ]
        self.three = [(i2, along_three(grid, value, m)) for i2, m, value in sends]
        return [value for _, _, value in sends]

    def add_three(self):
        if not self.path:
            return []
        grid = self.grid
        every = slice(0, grid.nz)
        sends = [self.terms(0, m, every).astype(BF) for m in range(1, grid.side)]
        self.two = [along_two(grid, sends[m - 1], m) for m in range(1, grid.side)]
        return sends

    def add_two(self):
        if not self.path:
            return []
        grid = self.grid
        sends = [self.terms(0, 0, slice(m, m + 1))[0].astype(BF) for m in range(1, grid.nz)]
        self.z = [
            permute(sends[m - 1], grid, lambda c: grid.z_mask(m)) for m in range(1, grid.nz)
        ]
        return sends

    def add_z(self):
        if not self.path:
            rows = [v.reshape(-1, v.shape[-1]).astype(F32) for v in self.keep]
            return jnp.concatenate(
                [lax.psum_scatter(v, AXES, scatter_dimension=0, tiled=True) for v in rows]
            )
        total = self.terms(0, 0, slice(0, 1))[0]
        for got in self.z:
            total = total + got.astype(F32)
        return total


def params(**more):
    return pltpu.CompilerParams(vmem_limit_bytes=VMEM_LIMIT, **more)


def cost(macs, bytes_accessed, trans=0):
    return pl.CostEstimate(
        flops=2 * macs // COST, bytes_accessed=bytes_accessed // COST, transcendentals=trans // COST
    )


def rows_spec(width, tile=TILE):
    return pl.BlockSpec((tile, width), lambda i: (i, 0))


def whole(shape):
    zeros = (0,) * len(shape)
    return pl.BlockSpec(shape, lambda *i: zeros)


def fixed(*shape):
    zeros = (0,) * len(shape)
    return pl.BlockSpec(shape, lambda i: zeros)


def norm_rows(values):
    center = values - jnp.mean(values, axis=-1, keepdims=True)
    inverse = lax.rsqrt(jnp.mean(center * center, axis=-1, keepdims=True) + epsilon)
    return center * inverse, inverse


def norm_back(upstream, normed, inverse, gain):
    u = upstream * gain
    centered = u - jnp.mean(u, axis=-1, keepdims=True)
    return inverse * (centered - normed * jnp.mean(u * normed, axis=-1, keepdims=True))


def gelu_pair(u):
    phi = 0.5 + 0.5 * lax.erf(u * math.sqrt(0.5))
    density = jnp.exp(-0.5 * (u * u))
    return u * phi, phi + (u * (1.0 / math.sqrt(2.0 * math.pi))) * density


def load_sequences(me_ref, mine, others, dest, sems):
    count = mine.shape[0] // 2
    half = mine.shape[1]
    core = me_ref[0] & 1
    copies = []
    for s in range(count):
        seq = me_ref[1 + s]
        for i, src in enumerate((mine, others)):
            at = s * 2 * half + (core ^ i) * half
            copies.append(
                pltpu.make_async_copy(
                    src.at[seq], dest.at[pl.ds(pl.multiple_of(at, half), half)], sems.at[2 * s + i]
                )
            )
    for copy in copies:
        copy.start()
    return copies


def store_sequences(me_ref, src, mine, others, sems):
    count, half = others.shape[0], others.shape[1]
    core = me_ref[0] & 1
    copies = []
    for s in range(count):
        for i, dest in enumerate((mine.at[me_ref[1 + s]], others.at[s])):
            at = s * 2 * half + (core ^ i) * half
            copies.append(
                pltpu.make_async_copy(
                    src.at[pl.ds(pl.multiple_of(at, half), half)], dest, sems.at[2 * s + i]
                )
            )
    for copy in copies:
        copy.start()
    return copies


def quarter_order(grid, me_ref, pieces, i):
    if len(pieces) == 1:
        return i
    lines = grid.nz // 4
    return (i * lines ^ me_ref[0] // (2 * grid.side * grid.side)) // lines


def qkv_kernel(grid, me_ref, vec_ref, mine, others, *rest):
    pieces, (out_hbm, x_hbm, w, x, out, wsem, xsem, osem) = rest[:-8], rest[-8:]
    rows, width = x.shape
    loads = load_sequences(me_ref, mine, others, x, xsem)
    blocks = grid.devices // 4
    start_natural(grid, me_ref, pieces, w, wsem, 0, 3 * blocks)
    for copy in loads:
        copy.wait()
    copy_x = pltpu.make_async_copy(x, x_hbm, osem.at[3])
    copy_x.start()

    def store(part):
        cols = pl.ds(pl.multiple_of(part * width, width), width)
        return pltpu.make_async_copy(out.at[:, cols], out_hbm.at[:, cols], osem.at[part])

    @pl.loop(0, 4)
    def _(i):
        part = quarter_order(grid, me_ref, pieces, i)

        @pl.when(part < 3)
        def _():
            wait_natural(grid, pieces, w, wsem, part * blocks, blocks, 0, 3 * blocks)
            cols = pl.ds(pl.multiple_of(part * width, width), width)
            bias = vec_ref[:, pl.ds(pl.multiple_of(part // 2 * width, width), width)]
            bias = jnp.where(part == 1, 0.0, bias)
            scale = jnp.where(part == 0, (width // H) ** -0.5, 1.0)
            out[:, cols] = ((nt(x[...], w[cols, :]) + bias) * scale).astype(BF)
            store(part).start()

    for part in range(3):
        store(part).wait()
    copy_x.wait()


def qkv_call(grid, me, vec, mine, others, pieces):
    width = mine.shape[2]
    rows = mine.shape[0] * mine.shape[1]
    return pl.pallas_call(
        lambda *r: qkv_kernel(grid, *r),
        in_specs=[SMEM, VMEM, ANY, ANY] + [ANY] * len(pieces),
        out_specs=[ANY, ANY],
        out_shape=[
            jax.ShapeDtypeStruct((rows, 3 * width), BF),
            jax.ShapeDtypeStruct((rows, width), BF),
        ],
        scratch_shapes=[
            pltpu.VMEM((3 * width, width), BF),
            pltpu.VMEM((rows, width), BF),
            pltpu.VMEM((rows, 3 * width), BF),
            pltpu.SemaphoreType.DMA((grid.devices,)),
            pltpu.SemaphoreType.DMA((mine.shape[0],)),
            pltpu.SemaphoreType.DMA((4,)),
        ],
        compiler_params=params(),
        cost_estimate=cost(rows * width * 3 * width, 12 << 20),
        name="qkv",
    )(me, vec, mine, others, *pieces)


def vector_refs(vec_ref, width):
    tail = 3 * width + FF
    found = [vec_ref[:, 2 * width : 3 * width], vec_ref[:, 3 * width : tail]]
    return found + [vec_ref[:, tail + i * width : tail + (i + 1) * width] for i in range(5)]


def live_blocks(live_len, length, body):
    size = min(128, length)
    count = (live_len + (size - 1)) // size
    for n in range(1, length // size + 1):
        pl.when(count == n)(lambda n=n: body(n * size))


def attend_kernel(grid, npieces, seq, len_ref, me_ref, q_ref, k_ref, v_ref, x_ref, vec_ref, *rest):
    pieces = rest[:npieces]
    quarter = grid.devices // 4
    ctx_ref, lse_ref, normed_ref, inv_ref, hid_ref, w, sems = rest[-7:]
    turn = pl.program_id(0)

    @pl.when(turn == 0)
    def _():
        start_natural(grid, me_ref, pieces, w, sems, 3 * quarter)

    live_len = len_ref[seq]
    length, pair = q_ref.shape
    half = pair // 2

    def attend(keys):
        q, k, v = q_ref[...], k_ref[0:keys, :], v_ref[0:keys, :]
        lane = lax.broadcasted_iota(jnp.int32, (length, pair), 1)
        live = lax.broadcasted_iota(jnp.int32, (1, keys), 1) < live_len
        outs, stats = [], []
        for h in (0, 1):
            mine = (lane >= half) if h else (lane < half)
            s = nt(jnp.where(mine, q, jnp.zeros_like(q)), k)
            s = jnp.where(live, s, masked_score)
            top = jnp.max(s, axis=-1, keepdims=True)
            p = jnp.exp(s - top)
            total = jnp.sum(p, axis=-1, keepdims=True)
            outs.append(nn(p.astype(BF), v) / total)
            stats.append(top + jnp.log(total))
        ctx = jnp.where(lane < half, outs[0], outs[1]).astype(BF)
        ctx_ref[:, pl.ds(pl.multiple_of(turn * pair, pair), pair)] = ctx
        turned = jnp.where(lane < half, stats[0], stats[1]).T
        lse_ref[0] = jnp.concatenate([turned[0:1], turned[half : half + 1]], axis=0)

    live_blocks(live_len, length, attend)

    @pl.when(turn == pl.num_programs(0) - 1)
    def _():
        wait_natural(grid, pieces, w, sems, 3 * quarter, quarter, 3 * quarter)
        bo, _, _, g1, e1, _, _ = vector_refs(vec_ref, x_ref.shape[1])
        r = x_ref[...].astype(F32) + (nt(ctx_ref[...], w[...]) + bo)
        normed, inverse = norm_rows(r)
        normed_ref[...] = normed
        inv_ref[...] = inverse
        hid_ref[...] = (normed * g1 + e1).astype(BF)


def attend_call(grid, me, lens, qkv, x, vec, pieces, seqs, seq, before, deps):
    rows, width = x.shape
    length = rows // seqs
    pairs = H // 2
    pw = width // pairs
    at = lambda part: pl.BlockSpec((length, pw), lambda p: (seq, part * pairs + p))
    seq_rows = lambda w: pl.BlockSpec((length, w), lambda p: (seq, 0))
    first = 7 + len(pieces)
    return pl.pallas_call(
        lambda *r: attend_kernel(grid, len(pieces), seq, *r),
        grid=(pairs,),
        in_specs=[SMEM, SMEM, at(0), at(1), at(2), seq_rows(width), whole(vec.shape)]
        + [ANY] * (len(pieces) + len(before) + len(deps)),
        out_specs=[
            seq_rows(width),
            pl.BlockSpec((1, 2, length), lambda p: (seq * pairs + p, 0, 0)),
            seq_rows(width),
            seq_rows(1),
            seq_rows(width),
        ],
        out_shape=[
            jax.ShapeDtypeStruct((rows, width), BF),
            jax.ShapeDtypeStruct((seqs * pairs, 2, length), F32),
            jax.ShapeDtypeStruct((rows, width), F32),
            jax.ShapeDtypeStruct((rows, 1), F32),
            jax.ShapeDtypeStruct((rows, width), BF),
        ],
        scratch_shapes=[
            pltpu.VMEM((width, width), BF),
            pltpu.SemaphoreType.DMA((grid.devices,)),
        ],
        input_output_aliases={first + i: i for i in range(len(before))},
        compiler_params=params(),
        cost_estimate=cost(8 * H * length * length * (width // H), 9 << 20, H * length * length),
        name="attend",
    )(lens, me, qkv, qkv, qkv, x, vec, *pieces, *before, *deps)


PARTS = 4


def ffn_kernel(grid, per, me_ref, vec_ref, inv_ref, h_hbm, normed_hbm, dy_mine, dy_others, *rest):
    npieces = len(rest) - 22 - (8 if is_path(grid, per) else 2)
    pieces = rest[:npieces]
    out_mine, out_others, dres_hbm, datt_hbm, sums_ref, db1_ref = rest[npieces : npieces + 6]
    grads = rest[npieces + 6 : -16]
    (w, h, normed, dy, act, gp, acc, dres, dbr, out, dpre, stage, wsem, isem, osem, dsem) = rest[-16:]
    rows, width = h.shape
    units = w.shape[0] // 2
    size = units // PARTS
    tiles = rows // TILE
    me = me_ref[0]
    core = me & 1

    _, _, b2, g1, e1, g2, e2 = vector_refs(vec_ref, width)
    loads = [
        pltpu.make_async_copy(src, dst, isem.at[i])
        for i, (src, dst) in enumerate(((h_hbm, h), (normed_hbm, normed)))
    ]
    loads[0].start()
    half = grid.devices // 2
    start_natural(grid, me_ref, pieces, w, wsem, order=lambda j: (j % half // (half // PARTS), j))
    loads[1].start()
    loads += load_sequences(me_ref, dy_mine, dy_others, dy, dsem)
    loads[0].wait()

    def tile(r):
        return pl.ds(pl.multiple_of(r * TILE, TILE), TILE)

    def natural_part(part):
        if len(pieces) == 1:
            return part
        return part ^ (me % half // (half // PARTS))

    def span(start, count):
        return pl.ds(pl.multiple_of(start, count), count)

    for part in range(PARTS):
        there = natural_part(part)
        for base in (0, half):
            wait_natural(
                grid, pieces, w, wsem, base + there * (half // PARTS), half // PARTS
            )
        here = slice(part * size, (part + 1) * size)
        up, down = span(there * size, size), span(units + there * size, size)
        a, slope = gelu_pair(nt(h[...], w[up, :]) + vec_ref[:, span(3 * width + there * size, size)])
        a = a.astype(BF)
        act[:, here] = a
        gp[:, here] = slope.astype(BF)
        more = nn(a, w[down, :])
        if part == 0:
            acc[...] = more
        else:
            acc[...] += more

    for copy in loads[1:]:
        copy.wait()
    sums_ref[...] = jnp.zeros_like(sums_ref)

    @pl.loop(0, tiles)
    def _(r):
        at = tile(r)
        hidden = normed[at, :] * g1 + e1
        value = hidden + (acc[at, :] + b2)
        n, inverse = norm_rows(value)
        out[at, :] = (n * g2 + e2).astype(BF)
        up = dy[at, :].astype(F32)
        d = norm_back(up, n, inverse, g2)
        low = d.astype(BF)
        dres[at, :] = d
        dbr[at, :] = low
        sums_ref[0:1] += jnp.sum(up * n, axis=0, keepdims=True)
        sums_ref[1:2] += jnp.sum(up, axis=0, keepdims=True)
        sums_ref[2:3] += jnp.sum(low.astype(F32), axis=0, keepdims=True)

    out_copies = store_sequences(me_ref, out, out_mine, out_others, dsem)

    path = is_path(grid, per)
    blocks = size // per
    pending = [[], []]

    def emit(part, side, value):
        slot, there = part % 2, natural_part(part)
        stage[slot, side] = value
        if not path:
            copy = pltpu.make_async_copy(
                stage.at[slot, side],
                grads[0].at[span(side * units + there * size, size)],
                osem.at[slot, side, 0],
            )
            copy.start()
            pending[slot].append(copy)
            return
        spread = 2 * grid.side * grid.side
        iz = (side * half ^ me & half) // spread + part // 2
        for x in (0, 1):
            for other in (0, 1):
                label = 2 * x + other
                here = label ^ (me & 3)
                src = stage.at[slot, side, pl.ds(pl.multiple_of(here * per, per), per)]
                pending[slot].append(
                    start_store(core, src, grads, x, part % 2, other, iz, osem.at[slot, side, label])
                )

    for part in range(PARTS):
        there = natural_part(part)
        here = slice(part * size, (part + 1) * size)
        up, down = span(there * size, size), span(units + there * size, size)
        d = (nt(dbr[...], w[down, :]) * gp[:, here].astype(F32)).astype(BF)
        dpre[...] = d
        db1_ref[:, span(there * size, size)] = jnp.sum(d.astype(F32), axis=0, keepdims=True)
        more = nn(d, w[up, :])
        if part == 0:
            acc[...] = more
        else:
            acc[...] += more
        for copy in pending[part % 2]:
            copy.wait()
        pending[part % 2] = []
        emit(part, 0, tn(dpre[...], h[...]).astype(BF))
        emit(part, 1, tn(act[:, here], dbr[...]).astype(BF))

    def stores(r):
        return [
            pltpu.make_async_copy(dres.at[tile(r)], dres_hbm.at[tile(r)], isem.at[1]),
            pltpu.make_async_copy(out.at[tile(r)], datt_hbm.at[tile(r)], isem.at[2]),
        ]

    for copy in out_copies:
        copy.wait()

    @pl.loop(0, tiles)
    def _(r):
        at = tile(r)
        dhid = dres[at, :] + acc[at, :]
        n = normed[at, :]
        d = norm_back(dhid, n, inv_ref[at, :], g1)
        low = d.astype(BF)
        dres[at, :] = d
        out[at, :] = low
        sums_ref[3:4] += jnp.sum(dhid * n, axis=0, keepdims=True)
        sums_ref[4:5] += jnp.sum(dhid, axis=0, keepdims=True)
        sums_ref[5:6] += jnp.sum(low.astype(F32), axis=0, keepdims=True)
        for copy in stores(r):
            copy.start()

    @pl.loop(0, tiles)
    def _(r):
        for copy in stores(r):
            copy.wait()

    for copy in pending[0] + pending[1]:
        copy.wait()


def ffn_call(grid, me, vec, inv, h, normed, dy_mine, dy_others, pieces, per):
    rows, width = h.shape
    total = grid.devices * per
    units = total // 2
    size = units // PARTS
    paths = path_shapes(grid, grid.devices, per, width)
    return pl.pallas_call(
        lambda *r: ffn_kernel(grid, per, *r),
        in_specs=[SMEM, VMEM, VMEM, ANY, ANY, ANY, ANY] + [ANY] * len(pieces),
        out_specs=[ANY, ANY, ANY, ANY, VMEM, VMEM] + [ANY] * len(paths),
        out_shape=[
            jax.ShapeDtypeStruct(dy_mine.shape, BF),
            jax.ShapeDtypeStruct((dy_mine.shape[0] // 2,) + dy_mine.shape[1:], BF),
            jax.ShapeDtypeStruct((rows, width), F32),
            jax.ShapeDtypeStruct((rows, width), BF),
            jax.ShapeDtypeStruct((8, width), F32),
            jax.ShapeDtypeStruct((1, units), F32),
        ]
        + paths,
        scratch_shapes=[
            pltpu.VMEM((total, width), BF),
            pltpu.VMEM((rows, width), BF),
            pltpu.VMEM((rows, width), F32),
            pltpu.VMEM((rows, width), BF),
            pltpu.VMEM((rows, units), BF),
            pltpu.VMEM((rows, units), BF),
            pltpu.VMEM((rows, width), F32),
            pltpu.VMEM((rows, width), F32),
            pltpu.VMEM((rows, width), BF),
            pltpu.VMEM((rows, width), BF),
            pltpu.VMEM((rows, size), BF),
            pltpu.VMEM((2, 2, size, width), BF),
            pltpu.SemaphoreType.DMA((grid.devices,)),
            pltpu.SemaphoreType.DMA((3,)),
            pltpu.SemaphoreType.DMA((2, 2, max(size // per, 2))),
            pltpu.SemaphoreType.DMA((dy_mine.shape[0],)),
        ],
        compiler_params=params(),
        cost_estimate=cost(6 * rows * width * units, 40 << 20, 2 * rows * units),
        name="ffn",
    )(me, vec, inv, h, normed, dy_mine, dy_others, *pieces)


def out_back_kernel(grid, npieces, me_ref, datt_hbm, ctx_hbm, *rest):
    pieces = rest[:npieces]
    dctx_hbm, grad_hbm, w, datt, ctx, dctx, grad, sems, isem, osem = rest[-10:]
    first = 3 * grid.devices // 4
    loads = [
        pltpu.make_async_copy(datt_hbm, datt, isem.at[0]),
        pltpu.make_async_copy(ctx_hbm, ctx, isem.at[1]),
    ]
    loads[0].start()
    start_natural(grid, me_ref, pieces, w, sems, first)
    loads[1].start()
    loads[0].wait()
    wait_natural(grid, pieces, w, sems, first, grid.devices - first, first)
    dctx[...] = nn(datt[...], w[...]).astype(BF)
    stores = [
        pltpu.make_async_copy(dctx, dctx_hbm, osem.at[0]),
        pltpu.make_async_copy(grad, grad_hbm, osem.at[1]),
    ]
    stores[0].start()
    loads[1].wait()
    grad[...] = tn(datt[...], ctx[...]).astype(BF)
    stores[1].start()
    for copy in stores:
        copy.wait()


def out_back_call(grid, me, datt, ctx, pieces, deps):
    rows, width = ctx.shape
    return pl.pallas_call(
        lambda *r: out_back_kernel(grid, len(pieces), *r),
        in_specs=[SMEM, ANY, ANY] + [ANY] * (len(pieces) + len(deps)),
        out_specs=[ANY, ANY],
        out_shape=[
            jax.ShapeDtypeStruct((rows, width), BF),
            jax.ShapeDtypeStruct((width, width), BF),
        ],
        scratch_shapes=[
            pltpu.VMEM((width, width), BF),
            pltpu.VMEM((rows, width), BF),
            pltpu.VMEM((rows, width), BF),
            pltpu.VMEM((rows, width), BF),
            pltpu.VMEM((width, width), BF),
            pltpu.SemaphoreType.DMA((grid.devices,)),
            pltpu.SemaphoreType.DMA((2,)),
            pltpu.SemaphoreType.DMA((2,)),
        ],
        compiler_params=params(),
        cost_estimate=cost(2 * rows * width * width, 12 << 20),
        name="out_back",
    )(me, datt, ctx, *pieces, *deps)


def attend_back_kernel(seq, len_ref, q_ref, k_ref, v_ref, d_ref, lse_ref, *rest):
    dz_ref, db_ref, _ = rest[-3:]
    live_len = len_ref[seq]
    length, pair = q_ref.shape
    half = pair // 2

    def back(keys):
        q, k, v, d = q_ref[...], k_ref[0:keys, :], v_ref[0:keys, :], d_ref[...]
        first = lax.broadcasted_iota(jnp.int32, (length, pair), 1) < half
        live = lax.broadcasted_iota(jnp.int32, (keys, 1), 0) < live_len
        zero = jnp.zeros_like(q)
        q2, d2 = (
            jnp.concatenate([jnp.where(first, t, zero), jnp.where(first, zero, t)]) for t in (q, d)
        )
        log_total = jnp.concatenate([lse_ref[0, 0:1, :], lse_ref[0, 1:2, :]], axis=1)
        p = jnp.where(live, jnp.exp(nt(k, q2) - log_total), 0.0)
        dp = nt(v, d2)
        inner = jnp.sum(p * dp, axis=0, keepdims=True)
        ds = (p * (dp - inner)).astype(BF)
        dv = nn(p.astype(BF), d2).astype(BF)
        dk = nn(ds, q2).astype(BF)
        turned = nn(k.T, ds)
        dq = jnp.concatenate([turned[:half, :length], turned[half:, length:]]).T
        dq = (dq.astype(BF).astype(F32) * half**-0.5).astype(BF)
        dz_ref[0] = dq
        dz_ref[1, 0:keys] = dk
        dz_ref[2, 0:keys] = dv
        if keys < length:
            dead = jnp.zeros((length - keys, pair), BF)
            dz_ref[1, keys:length] = dead
            dz_ref[2, keys:length] = dead
        db_ref[0:1] = jnp.sum(dq.astype(F32), axis=0, keepdims=True)
        db_ref[1:2] = jnp.sum(dv.astype(F32), axis=0, keepdims=True)

    live_blocks(live_len, length, back)


def attend_back_call(lens, qkv, dctx, lse, seqs, seq, dz, carry, deps):
    rows, width = dctx.shape
    length = rows // seqs
    pairs = H // 2
    pw = width // pairs
    at = lambda part: pl.BlockSpec((length, pw), lambda p: (seq, part * pairs + p))
    more = [carry] + ([] if dz is None else [dz]) + list(deps)
    return pl.pallas_call(
        lambda *r: attend_back_kernel(seq, *r),
        grid=(pairs,),
        in_specs=[
            SMEM,
            at(0),
            at(1),
            at(2),
            at(0),
            pl.BlockSpec((1, 2, length), lambda p: (seq * pairs + p, 0, 0)),
        ]
        + [ANY] * len(more),
        out_specs=[
            pl.BlockSpec((3, length, pw), lambda p: (0, seq, p)),
            pl.BlockSpec((2, pw), lambda p: (0, p)),
            ANY,
        ],
        out_shape=[
            jax.ShapeDtypeStruct((3, rows, width), BF),
            jax.ShapeDtypeStruct((2, width), F32),
            jax.ShapeDtypeStruct(carry.shape, carry.dtype),
        ],
        input_output_aliases={6: 2} if dz is None else {6: 2, 7: 0},
        compiler_params=params(),
        cost_estimate=cost(
            20 * H * length * length * (width // H), 6 << 20, H * length * length
        ),
        name="attend_back",
    )(lens, qkv, qkv, qkv, dctx, lse, *more)


def attn_grad_kernel(
    grid, per, npieces, me_ref, sums, db1, db_a, db_b, dz_hbm, x_hbm, gout_hbm, dres_hbm, *rest
):
    pieces = rest[:npieces]
    count = 8 if is_path(grid, per) else 2
    grads, (mine, others) = rest[-13 - count : -13], rest[-13:-11]
    stage, dz, x, gout, line, total, w = rest[-11:-4]
    isem, osem, wsem, dsem = rest[-4:]
    rows, width = x.shape
    me = me_ref[0]
    core = me & 1
    blocks = grid.devices // 4
    path = is_path(grid, per)
    loads = [pltpu.make_async_copy(gout_hbm, gout, isem.at[4])]
    loads += [pltpu.make_async_copy(x_hbm, x, isem.at[3])]
    loads += [pltpu.make_async_copy(dz_hbm.at[p], dz.at[p], isem.at[p]) for p in range(3)]
    for copy in loads:
        copy.start()
    load_total = pltpu.make_async_copy(dres_hbm, total, isem.at[5])
    load_total.start()
    start_natural(grid, me_ref, pieces, w, wsem, 0, 3 * blocks)

    db = db_a[...] + db_b[...]
    tail = 3 * width + FF
    line[:, 0:width] = db[0:1]
    line[:, width : 2 * width] = db[1:2]
    line[:, 2 * width : 3 * width] = sums[5:6]
    line[:, 3 * width : tail] = db1[...]
    for i, row in enumerate((2, 3, 4, 0, 1)):
        line[:, tail + i * width : tail + (i + 1) * width] = sums[row : row + 1]
    count = line.shape[1] // grid.devices
    blank = jnp.zeros((8, width), F32)
    first_row = lax.broadcasted_iota(jnp.int32, (8, count), 0) == 0
    for d in range(grid.devices):
        values = jnp.where(first_row, line[:, d * count : (d + 1) * count], 0.0)
        values = jnp.concatenate([values, blank[:, count:]], axis=1).astype(BF)
        if path:
            stage[d, per : per + 8] = values
        else:
            grads[1][d] = values

    copies = []

    def emit(part, value):
        value = value.astype(BF)
        if not path:
            grads[0][part * width : (part + 1) * width, :] = value
            return
        stage[part * blocks : (part + 1) * blocks, 0:per] = value.reshape(blocks, per, width)
        iz = part ^ me // blocks
        for label in range(blocks):
            other, side_x, side_y = label & 1, label // 2 % 2, label // 4
            block = part * blocks + (label ^ (me & (blocks - 1)))
            copies.append(
                start_store(
                    core, stage.at[block], grads, side_x, side_y, other, iz, osem.at[part * blocks + label]
                )
            )

    loads[0].wait()
    emit(3, gout[...])
    loads[1].wait()
    for part in range(3):
        loads[2 + part].wait()
        emit(part, tn(dz[part], x[...]))
    load_total.wait()
    for part in range(3):
        wait_natural(grid, pieces, w, wsem, part * blocks, blocks, 0, 3 * blocks)
        total[...] += nn(dz[part], w[part * width : (part + 1) * width, :])
    for copy in store_sequences(me_ref, total, mine, others, dsem) + copies:
        copy.wait()


def attn_grad_call(grid, me, dz, x, gout, dres, vectors, pieces, per, shape, deps):
    rows, width = x.shape
    paths = path_shapes(grid, grid.devices, per, width)
    path = is_path(grid, per)
    if path:
        paths = [jax.ShapeDtypeStruct((p.shape[0], per + 8, width), BF) for p in paths]
    return pl.pallas_call(
        lambda *r: attn_grad_kernel(grid, per, len(pieces), *r),
        in_specs=[SMEM] + [VMEM] * len(vectors) + [ANY] * (4 + len(pieces) + len(deps)),
        out_specs=[ANY if path else VMEM] * len(paths) + [ANY, ANY],
        out_shape=paths
        + [
            jax.ShapeDtypeStruct(shape, F32),
            jax.ShapeDtypeStruct((shape[0] // 2,) + shape[1:], F32),
        ],
        scratch_shapes=[
            pltpu.VMEM((grid.devices, per + 8, width), BF),
            pltpu.VMEM((3, rows, width), BF),
            pltpu.VMEM((rows, width), BF),
            pltpu.VMEM((width, width), BF),
            pltpu.VMEM((1, 8 * width + FF), F32),
            pltpu.VMEM((rows, width), F32),
            pltpu.VMEM((3 * width, width), BF),
            pltpu.SemaphoreType.DMA((6,)),
            pltpu.SemaphoreType.DMA((grid.devices,)),
            pltpu.SemaphoreType.DMA((grid.devices,)),
            pltpu.SemaphoreType.DMA((shape[0],)),
        ],
        compiler_params=params(),
        cost_estimate=cost(6 * rows * width * width, 28 << 20),
        name="attn_grad",
    )(me, *vectors, dz, x, gout, dres, *pieces, *deps)


def gate(value, deps):
    return pl.pallas_call(
        lambda *r: None,
        in_specs=[ANY] * (1 + len(deps)),
        out_specs=ANY,
        out_shape=jax.ShapeDtypeStruct(value.shape, value.dtype),
        input_output_aliases={0: 0},
        compiler_params=params(),
        cost_estimate=cost(0, 0),
        name="gate",
    )(value, *deps)


def ordered_stack_kernel(count, *rest):
    for i in range(count):
        rest[-1][i] = rest[i][...]


def ordered_stack(parts, deps):
    return pl.pallas_call(
        lambda *r: ordered_stack_kernel(len(parts), *r),
        in_specs=[VMEM] * len(parts) + [ANY] * len(deps),
        out_specs=VMEM,
        out_shape=jax.ShapeDtypeStruct((len(parts),) + parts[0].shape, parts[0].dtype),
        compiler_params=params(),
        name="ordered_stack",
    )(*parts, *deps)


def adam_update(master, moment, second, grad, rate):
    moment_new = decay_rate * moment + (1.0 - decay_rate) * grad
    second_new = decay_rate * second + (1.0 - decay_rate) * grad * grad
    correction = 1.0 - decay_rate**STEP
    direction = moment_new / correction / (jnp.sqrt(second_new / correction) + adam_epsilon)
    master_new = master - rate * (direction + weight_decay * master)
    return (moment_new, second_new, master_new)


def join_sequences(mine, others, places):
    for s in range(others.shape[0]):
        mine = lax.dynamic_update_slice(mine, others[s : s + 1], (places[s], 0, 0))
    return mine


def share_sequences(lengths, core):
    count = lengths.shape[0]
    number = jnp.arange(count)
    longer = (lengths[None, :] > lengths[:, None]) | (
        (lengths[None, :] == lengths[:, None]) & (number[None, :] < number[:, None])
    )
    rank = jnp.sum(longer.astype(jnp.int32), axis=1)
    by_rank = jnp.sum((rank[None, :] == number[:, None]) * number[None, :], axis=1)
    sides = [[r for r in range(count) if (r + 1) // 2 % 2 == c] for c in (0, 1)]
    first, second = (jnp.stack([by_rank[r] for r in side]) for side in sides)
    mine = jnp.where(core == 0, first, second).astype(jnp.int32)
    other = jnp.where(core == 0, second, first).astype(jnp.int32)
    return mine, other


def local(
    tokens,
    cotangent,
    seq_lengths,
    slot_order,
    attn_weights,
    attn_moment,
    attn_second,
    ffn_weights,
    ffn_moment,
    ffn_second,
    vectors,
    vector_moment,
    vector_second,
):
    grid = Grid(lax.axis_size("dp"))
    core = lax.axis_index("seq")
    shard_index = lax.axis_index(AXES)
    me = shard_index.astype(jnp.int32).reshape(1)
    seq_count, half_len, width = tokens.shape
    seqs = seq_count // 2
    length = 2 * half_len
    rows = seqs * length
    per, ffn_per = attn_weights.shape[1], ffn_weights.shape[1]
    vec_per = vectors.shape[0]
    path = is_path(grid, per) and is_path(grid, ffn_per)

    slot_pick = (slot_order[0][:, None] == jnp.arange(seq_count)[None, :]).astype(jnp.int32)
    slot_len = jnp.sum(slot_pick * seq_lengths[0][None, :], axis=1)
    taken, left = share_sequences(slot_len, core)
    lens = jnp.sum((taken[:, None] == jnp.arange(seq_count)[None, :]) * slot_len[None, :], axis=1)
    me = jnp.concatenate([me, taken])

    vec_rows = jnp.zeros((8, width), BF)
    vec_rows = lax.dynamic_update_slice(vec_rows, vectors.astype(BF)[None, :], (0, 0))
    attn_block = jnp.concatenate([attn_weights.astype(BF).T, vec_rows])

    other_core = lambda value: permute(value, grid, lambda c: 1)
    tokens_other = other_core(tokens)
    if path:
        attn_parts = gather_z(grid, attn_block)
        ffn_block = ffn_weights.astype(BF).T
        ffn_parts = gather_z(grid, ffn_block)
        attn_z = ordered_stack(attn_parts, [ffn_block])
        attn_two = gather_two(grid, attn_z)
        attn_two = attn_two[:1] + [gate(t, ffn_parts[1:2]) for t in attn_two[1:]]
        attn_three = gather_three(grid, attn_two)
        ffn_z = ordered_stack(ffn_parts, attn_two[1:])
        ffn_two = gather_two(grid, ffn_z)
        weights = with_core(grid, attn_two + attn_three, [ffn_z])
        vec = natural_vectors(grid, weights, core, me[0], per, vec_per)
    else:
        whole_rows = lambda block: [lax.all_gather(block, AXES, axis=0, tiled=True)]
        weights = whole_rows(attn_block[:per])
        ffn_pieces = whole_rows(ffn_weights.astype(BF).T)
        ffn_two = []
        vec = lax.all_gather(attn_block[per:], AXES)[:, 0, :vec_per].reshape(1, -1).astype(F32)
    dy_other = other_core(cotangent)

    qkv, x = qkv_call(grid, me, vec, tokens, tokens_other, weights)
    fwd = attend_call(grid, me, lens, qkv, x, vec, weights, seqs, 0, [], [])
    ffn_two = ffn_two[:1] + [gate(t, fwd[:1]) for t in ffn_two[1:]]
    fwd = attend_call(grid, me, lens, qkv, x, vec, weights, seqs, 1, fwd, ffn_two[1:])
    ctx, lse, normed, inv, hidden = fwd
    if path:
        ffn_three = gather_three(grid, ffn_two)
        ffn_three = ffn_three[:1] + [gate(t, fwd[:1]) for t in ffn_three[1:]]
        ffn_pieces = with_core(grid, ffn_two + ffn_three, [])
    out, out_other, dres_one, datt, sums, db1, *grads_f = ffn_call(
        grid, me, vec, inv, hidden, normed, cotangent, dy_other, ffn_pieces, ffn_per
    )
    layer_out = join_sequences(out, other_core(out_other), left)

    sums_f = Sums(grid, path, grads_f)
    sends = sums_f.add_core()
    dctx, gout = out_back_call(grid, me, datt, ctx, weights, sends)
    dz, db_a, sums_f.keep[1] = attend_back_call(
        lens, qkv, dctx, lse, seqs, 0, None, sums_f.keep[1], sends
    )
    sends = sums_f.add_three()
    dz, db_b, sums_f.keep[0] = attend_back_call(
        lens, qkv, dctx, lse, seqs, 1, dz, sums_f.keep[0], sends
    )
    sends = sums_f.add_two()
    *grads_c, dx, dx_other = attn_grad_call(
        grid, me, dz, x, gout, dres_one, [sums, db1, db_a, db_b], weights, per, tokens.shape, sends
    )
    if path:
        grads_c[7] = gate(grads_c[7], sums_f.z[1:2])
    sums_c = Sums(grid, path, grads_c)
    sums_c.add_core()
    ffn_sum = sums_f.add_z()
    sums_c.add_three()
    sums_c.keep[0] = gate(sums_c.keep[0], [ffn_sum])
    input_grad = join_sequences(dx, other_core(dx_other), left)
    sums_c.add_two()
    attn_sum = sums_c.add_z()

    vector_sum = attn_sum[per, :vec_per]
    attn_sum = attn_sum[:per].T
    ffn_sum = ffn_sum[:ffn_per].T

    attn_cols = shard_index * per + jnp.arange(per)
    attn_rate = jnp.where(
        attn_cols < 2 * width, math.sqrt(2.0), jnp.where(attn_cols < 3 * width, 1.5, 1.8)
    ) * width ** (-0.5)
    ffn_cols = shard_index * ffn_per + jnp.arange(ffn_per)
    ffn_rate = jnp.where(ffn_cols < FF, width ** (-0.5), 1.5 * FF ** (-0.5))
    attn_m, attn_v, attn_new = adam_update(
        attn_weights, attn_moment, attn_second, attn_sum, attn_rate[None, :]
    )
    ffn_m, ffn_v, ffn_new = adam_update(
        ffn_weights, ffn_moment, ffn_second, ffn_sum, ffn_rate[None, :]
    )
    vec_m, vec_v, vec_new = adam_update(
        vectors, vector_moment, vector_second, vector_sum, vector_rate
    )
    return (
        layer_out,
        input_grad,
        attn_m,
        attn_v,
        attn_new,
        attn_new.astype(BF),
        ffn_m,
        ffn_v,
        ffn_new,
        ffn_new.astype(BF),
        vec_m,
        vec_v,
        vec_new,
        vec_new.astype(BF),
    )


def solution(mesh):
    columns = P(None, AXES)
    flat = P(AXES)
    rows = P("dp", "seq", None)
    placed = (rows, rows, P("dp", None), P("dp", None)) + (columns,) * 6 + (flat,) * 3
    return jax.shard_map(
        local,
        mesh=mesh,
        in_specs=placed,
        out_specs=(rows, rows) + (columns,) * 8 + (flat,) * 4,
        check_vma=False,
    )
```

profile of v0, /device:TPU:0, one launch (start us, length us, event | category | flops | bytes accessed | tf_op | source)
XLA Modules:
  0.0 275.3 jit_solution(5099588527183600153)
XLA Ops:
  2.4 3.1 %collective-permute-start = (bf16[104,768]{1,0:T(8,128)(2,1)S(1)}, bf16[104,768]{1,0:T(8,128)(2,1)S(1)}, u32[]{:S(2)}, u32[]{:S(2)}) collective-permute-start(bf16[104,768]{1,0:T(8,128)(2,1)S(1)} %fusion.10.r_0_), channel_id=1, source_target_pairs={{0,8},{1,9},{2,10},{3,11},{4,12},{5,13},{6,14},{7,15},{8,0},{9,1},... | collective-permute-start | bytes 479240 | tf_op jit(solution)/shard_map/ppermute | solution.py:72
  5.5 2.6 collective-permute-start.1
  10.1 3.5 %collective-permute-start.4 = (bf16[192,768]{1,0:T(8,128)(2,1)S(1)}, bf16[192,768]{1,0:T(8,128)(2,1)S(1)}, u32[]{:S(2)}, u32[]{:S(2)}) collective-permute-start(bf16[192,768]{1,0:T(8,128)(2,1)S(1)} %convert_bitcast_fusion.r_4_.r_0_), channel_id=1, source_target_pairs={{0,16},{1,17},{2,18},{3,19},{4,20},{5,21},{6,22},{7,23},{8,24},{9,... | collective-permute-start | bytes 884744 | tf_op jit(solution)/shard_map/ppermute | solution.py:72
  14.0 3.1 %collective-permute-start.5 = (bf16[192,768]{1,0:T(8,128)(2,1)S(1)}, bf16[192,768]{1,0:T(8,128)(2,1)S(1)}, u32[]{:S(2)}, u32[]{:S(2)}) collective-permute-start(bf16[192,768]{1,0:T(8,128)(2,1)S(1)} %convert_bitcast_fusion.r_4_.r_0_), channel_id=1, source_target_pairs={{0,24},{1,25},{2,26},{3,27},{4,28},{5,29},{6,30},{7,31},{8,16},{9,... | collective-permute-start | bytes 884744 | tf_op jit(solution)/shard_map/ppermute | solution.py:72
  17.1 3.2 %collective-permute-done.1.r_2_ = bf16[104,768]{1,0:T(8,128)(2,1)S(1)} collective-permute-done((bf16[104,768]{1,0:T(8,128)(2,1)S(1)}, bf16[104,768]{1,0:T(8,128)(2,1)S(1)}, u32[]{:S(2)}, u32[]{:S(2)}) %collective-permute-start.1) | collective-permute-done | bytes 159776 | tf_op jit(solution)/shard_map/ppermute | solution.py:72
  21.6 2.0 ordered_stack.2.r_0_
  23.6 1.5 collective-permute-start.6
  25.1 1.5 collective-permute-start.7
  27.4 1.4 broadcast_select_fusion.3
  30.0 9.8 %collective-permute-done.6.r_0_ = bf16[4,104,768]{2,1,0:T(8,128)(2,1)S(1)} collective-permute-done((bf16[4,104,768]{2,1,0:T(8,128)(2,1)}, bf16[4,104,768]{2,1,0:T(8,128)(2,1)S(1)}, u32[]{:S(2)}, u32[]{:S(2)}) %collective-permute-start.6) | collective-permute-done | bytes 639008 | tf_op jit(solution)/shard_map/ppermute | solution.py:72
  41.5 1.2 collective-permute-done.4.r_2_
  44.1 2.3 ordered_stack.3.r_1_.r_7_
  48.3 4.5 %collective-permute-done.8.r_7_.r_10_.r_6_.r_12_ = bf16[4,104,768]{2,1,0:T(8,128)(2,1)S(1)} collective-permute-done((bf16[4,104,768]{2,1,0:T(8,128)(2,1)}, bf16[4,104,768]{2,1,0:T(8,128)(2,1)S(1)}, u32[]{:S(2)}, u32[]{:S(2)}) %collective-permute-start.8) | collective-permute-done | bytes 639008 | tf_op jit(solution)/shard_map/ppermute | solution.py:72
  54.2 2.0 collective-permute-done.12.r_11_.r_14_.r_10_.r_16_
  59.0 9.2 %qkv.1 = (bf16[1024,2304]{1,0:T(8,128)(2,1)}, bf16[1024,768]{1,0:T(8,128)(2,1)}) custom-call(s32[3]{0:T(128)} %pad_add_fusion.1.r_0_.r_1_, f32[1,9216]{1,0:T(1,128)} %reshape.78.r_1_.r_6_, bf16[4,256,768]{2,1,0:T(8,128)(2,1)} %r_2_.1, bf16[4,256,768]{2,1,0:T(8,128)(2,1)} %collective-permute-done.13.r_3_, bf16[4,104,768]{2,1,0:T(8,128)(2,1)} %gate.7.r_4_.r_7_.r_3_.r_9_, ...), custom_call_target="tpu_custom_call" | custom-call | flops 226492416 | bytes 786432 | tf_op jit(solution)/shard_map/qkv/pallas_call | solution.py:399
  68.3 12.1 %attend.2 = (bf16[1024,768]{1,0:T(8,128)(2,1)}, f32[12,2,512]{2,1,0:T(2,128)}, f32[1024,768]{1,0:T(8,128)}, f32[1024,1]{1,0:T(8,128)}, bf16[1024,768]{1,0:T(8,128)(2,1)}) custom-call(s32[2]{0:T(128)} %fusion.19.r_0_, s32[3]{0:T(128)} %pad_add_fusion.1.r_0_.r_1_, bf16[1024,2304]{1,0:T(8,128)(2,1)} %get-tuple-element.58.r_2_.r_3_.r_4_.r_1_, ...), custom_call_target="tpu_custom_call" | custom-call | flops 201326592 | bytes 589824 | tf_op jit(solution)/shard_map/attend/pallas_call | solution.py:488
  80.4 2.1 collective-permute-start.17
  83.5 10.4 %attend.3 = (bf16[1024,768]{1,0:T(8,128)(2,1)}, f32[12,2,512]{2,1,0:T(2,128)}, f32[1024,768]{1,0:T(8,128)}, f32[1024,1]{1,0:T(8,128)}, bf16[1024,768]{1,0:T(8,128)(2,1)}) custom-call(s32[2]{0:T(128)} %fusion.19.r_0_, s32[3]{0:T(128)} %pad_add_fusion.1.r_0_.r_1_, ...), custom_call_target="tpu_custom_call", output_to_operand_aliasing={{0}: (15, {}), {1}: (16, {}), {2}: (17, {}), {3}: (18, {}),... | custom-call | flops 201326592 | bytes 589824 | tf_op jit(solution)/shard_map/attend/pallas_call | solution.py:488
  93.9 3.0 %collective-permute-done.17.r_0_ = bf16[4,192,768]{2,1,0:T(8,128)(2,1)S(1)} collective-permute-done((bf16[4,192,768]{2,1,0:T(8,128)(2,1)}, bf16[4,192,768]{2,1,0:T(8,128)(2,1)S(1)}, u32[]{:S(2)}, u32[]{:S(2)}) %collective-permute-start.17) | collective-permute-done | bytes 1179680 | tf_op jit(solution)/shard_map/ppermute | solution.py:72
  98.0 3.0 %collective-permute-done.21.r_14_ = bf16[4,192,768]{2,1,0:T(8,128)(2,1)S(1)} collective-permute-done((bf16[4,192,768]{2,1,0:T(8,128)(2,1)}, bf16[4,192,768]{2,1,0:T(8,128)(2,1)S(1)}, u32[]{:S(2)}, u32[]{:S(2)}) %collective-permute-start.21) | collective-permute-done | bytes 1179680 | tf_op jit(solution)/shard_map/ppermute | solution.py:72
  102.0 47.2 %ffn.1 = (bf16[4,256,768]{2,1,0:T(8,128)(2,1)}, bf16[2,256,768]{2,1,0:T(8,128)(2,1)}, f32[1024,768]{1,0:T(8,128)}, bf16[1024,768]{1,0:T(8,128)(2,1)}, f32[8,768]...) custom-call(s32[3]{0:T(128)} %pad_add_fusion.1.r_0_.r_1_, ...), custom_call_target="tpu_custom_call" | custom-call | flops 1811939328 | bytes 2621440 | tf_op jit(solution)/shard_map/ffn/pallas_call | solution.py:681
  149.9 2.4 collective-permute-done.23
  152.4 1.7 add_convert_fusion.2.r_11_.r_7_
  154.0 2.1 collective-permute-start.26
  157.5 7.5 %out_back.1 = (bf16[1024,768]{1,0:T(8,128)(2,1)}, bf16[768,768]{1,0:T(8,128)(2,1)}) custom-call(s32[3]{0:T(128)} %pad_add_fusion.1.r_0_.r_1_, bf16[1024,768]{1,0:T(8,128)(2,1)} %get-tuple-element.73.r_1_, bf16[1024,768]{1,0:T(8,128)(2,1)} %get-tuple-element.68.r_1_.r_2_, bf16[4,104,768]{2,1,0:T(8,128)(2,1)} %gate.7.r_4_.r_7_.r_3_.r_9_, ...), custom_call_target="tpu_custom_call" | custom-call | flops 150994944 | bytes 786432 | tf_op jit(solution)/shard_map/out_back/pallas_call | solution.py:746
  165.0 13.7 %attend_back.2 = (bf16[3,1024,768]{2,1,0:T(8,128)(2,1)}, f32[2,768]{1,0:T(2,128)}, bf16[4,192,768]{2,1,0:T(8,128)(2,1)}) custom-call(s32[2]{0:T(128)} %fusion.19.r_0_, bf16[1024,2304]{1,0:T(8,128)(2,1)} %get-tuple-element.58.r_2_.r_3_.r_4_.r_1_, bf16[1024,2304]{1,0:T(8,128)(2,1)} %get-tuple-element.58.r_2_.r_3_.r_4_.r_1_, ...), custom_call_target="tpu_custom_call", output_to_operand_aliasing={{2}: (6, {})} | custom-call | flops 503316480 | bytes 393216 | tf_op jit(solution)/shard_map/attend_back/pallas_call | solution.py:814
  178.7 1.7 add_convert_fusion.r_8_
  181.5 9.1 %attend_back.3 = (bf16[3,1024,768]{2,1,0:T(8,128)(2,1)}, f32[2,768]{1,0:T(2,128)}, bf16[4,192,768]{2,1,0:T(8,128)(2,1)}) custom-call(s32[2]{0:T(128)} %fusion.19.r_0_, bf16[1024,2304]{1,0:T(8,128)(2,1)} %get-tuple-element.58.r_2_.r_3_.r_4_.r_1_, ...), custom_call_target="tpu_custom_call", output_to_operand_aliasing={{2}: (6, {}), {0}: (7, {})} | custom-call | flops 503316480 | bytes 393216 | tf_op jit(solution)/shard_map/attend_back/pallas_call | solution.py:814
  190.7 6.1 %collective-permute-done.29 = bf16[4,192,768]{2,1,0:T(8,128)(2,1)S(1)} collective-permute-done((bf16[4,192,768]{2,1,0:T(8,128)(2,1)S(1)}, bf16[4,192,768]{2,1,0:T(8,128)(2,1)S(1)}, u32[]{:S(2)}, u32[]{:S(2)}) %collective-permute-start.29) | collective-permute-done | bytes 1179680 | tf_op jit(solution)/shard_map/ppermute | solution.py:72
  196.7 2.4 fusion.9
  199.1 4.4 %collective-permute-start.32 = (bf16[192,768]{1,0:T(8,128)(2,1)S(1)}, bf16[192,768]{1,0:T(8,128)(2,1)S(1)}, u32[]{:S(2)}, u32[]{:S(2)}) collective-permute-start(bf16[192,768]{1,0:T(8,128)(2,1)S(1)} %get-tuple-element.132.r_18_), channel_id=1, source_target_pairs={{0,16},{1,17},{2,18},{3,19},{4,20},{5,21},{6,22},{7,23},{8,24},{9,... | collective-permute-start | bytes 884744 | tf_op jit(solution)/shard_map/ppermute | solution.py:72
  203.5 17.4 %attn_grad.1 = (bf16[4,104,768]{2,1,0:T(8,128)(2,1)}, bf16[4,104,768]{2,1,0:T(8,128)(2,1)}, bf16[4,104,768]{2,1,0:T(8,128)(2,1)}, bf16[4,104,768]{2,1,0:T(8,128)...) custom-call(s32[3]{0:T(128)} %pad_add_fusion.1.r_0_.r_1_, ...), custom_call_target="tpu_custom_call" | custom-call | flops 452984832 | bytes 1835008 | tf_op jit(solution)/shard_map/attn_grad/pallas_call | solution.py:924
  227.3 1.5 add_convert_fusion.4
  228.8 1.1 collective-permute-start.39
  229.9 1.8 slice_dynamic-update-slice_fusion.3
  231.7 1.8 slice_dynamic-update-slice_fusion.2
  233.5 2.0 collective-permute-start.33
  236.6 2.7 collective-permute-done.39
  240.6 2.8 %collective-permute-done.31 = bf16[192,768]{1,0:T(8,128)(2,1)S(1)} collective-permute-done((bf16[192,768]{1,0:T(8,128)(2,1)S(1)}, bf16[192,768]{1,0:T(8,128)(2,1)S(1)}, u32[]{:S(2)}, u32[]{:S(2)}) %collective-permute-start.31) | collective-permute-done | bytes 294944 | tf_op jit(solution)/shard_map/ppermute | solution.py:72
  244.2 4.7 %collective-permute-done.33 = bf16[192,768]{1,0:T(8,128)(2,1)S(1)} collective-permute-done((bf16[192,768]{1,0:T(8,128)(2,1)S(1)}, bf16[192,768]{1,0:T(8,128)(2,1)S(1)}, u32[]{:S(2)}, u32[]{:S(2)}) %collective-permute-start.33) | collective-permute-done | bytes 294944 | tf_op jit(solution)/shard_map/ppermute | solution.py:72
  248.9 2.9 %fusion.23 = (bf16[768,192]{0,1:T(8,128)(2,1)}, f32[768,192]{0,1:T(8,128)}, f32[768,192]{0,1:T(8,128)}, f32[768,192]{0,1:T(8,128)}, f32[192,768]{1,0:T(8,128)}) fusion(f32[768,192]{0,1:T(8,128)S(1)} %copy-done.14, f32[192]{0:T(256)S(1)} %compare_select_fusion, f32[768,192]{0,1:T(8,128)S(1)} %copy-done.32, f32[768,192]{0,1:T(8,128)S(1)} %copy-done.33, ...), kind=kLoop, calls=%fused_computation.93 | loop fusion | flops 4128768 | bytes 6488832 | tf_op jit(solution)/shard_map/convert_element_type | solution.py:1138
  252.7 2.9 %collective-permute-done.36 = bf16[4,104,768]{2,1,0:T(8,128)(2,1)} collective-permute-done((bf16[4,104,768]{2,1,0:T(8,128)(2,1)}, bf16[4,104,768]{2,1,0:T(8,128)(2,1)}, u32[]{:S(2)}, u32[]{:S(2)}) %collective-permute-start.36) | collective-permute-done | bytes 639008 | tf_op jit(solution)/shard_map/ppermute | solution.py:72
  255.7 1.5 fusion.11
  257.3 1.3 collective-permute-start.42
  258.5 3.1 %collective-permute-start.43 = (bf16[104,768]{1,0:T(8,128)(2,1)S(1)}, bf16[104,768]{1,0:T(8,128)(2,1)S(1)}, u32[]{:S(2)}, u32[]{:S(2)}) collective-permute-start(bf16[104,768]{1,0:T(8,128)(2,1)S(1)} %get-tuple-element.135), channel_id=1, source_target_pairs={{0,24},{1,25},{2,26},{3,27},{4,28},{5,29},{6,30},{7,31},{8,16},{9,... | collective-permute-start | bytes 479240 | tf_op jit(solution)/shard_map/ppermute | solution.py:72
  262.6 4.1 %collective-permute-done.41 = bf16[104,768]{1,0:T(8,128)(2,1)S(1)} collective-permute-done((bf16[104,768]{1,0:T(8,128)(2,1)S(1)}, bf16[104,768]{1,0:T(8,128)(2,1)S(1)}, u32[]{:S(2)}, u32[]{:S(2)}) %collective-permute-start.41) | collective-permute-done | bytes 159776 | tf_op jit(solution)/shard_map/ppermute | solution.py:72
  266.7 5.4 %collective-permute-done.42 = bf16[104,768]{1,0:T(8,128)(2,1)S(1)} collective-permute-done((bf16[104,768]{1,0:T(8,128)(2,1)S(1)}, bf16[104,768]{1,0:T(8,128)(2,1)S(1)}, u32[]{:S(2)}, u32[]{:S(2)}) %collective-permute-start.42) | collective-permute-done | bytes 159776 | tf_op jit(solution)/shard_map/ppermute | solution.py:72
  272.1 1.1 fusion.4
  (212 shorter events, 31.8 us)
Async XLA Ops:
  2.4 17.9 %copy-start.30 = (bf16[104,768]{1,0:T(8,128)(2,1)}, bf16[104,768]{1,0:T(8,128)(2,1)S(1)}, u32[]{:S(2)}) copy-start(bf16[104,768]{1,0:T(8,128)(2,1)S(1)} %fusion.10.r_0_) | copy-start | bytes 479236
  2.4 11.6 %collective-permute-start = (bf16[104,768]{1,0:T(8,128)(2,1)S(1)}, bf16[104,768]{1,0:T(8,128)(2,1)S(1)}, u32[]{:S(2)}, u32[]{:S(2)}) collective-permute-start(bf16[104,768]{1,0:T(8,128)(2,1)S(1)} %fusion.10.r_0_), channel_id=1, source_target_pairs={{0,8},{1,9},{2,10},{3,11},{4,12},{5,13},{6,14},{7,15},{8,0},{9,1},... | collective-permute-start | bytes 479240 | tf_op jit(solution)/shard_map/ppermute | solution.py:72
  5.5 14.8 %collective-permute-start.1 = (bf16[104,768]{1,0:T(8,128)(2,1)S(1)}, bf16[104,768]{1,0:T(8,128)(2,1)S(1)}, u32[]{:S(2)}, u32[]{:S(2)}) collective-permute-start(bf16[104,768]{1,0:T(8,128)(2,1)S(1)} %fusion.10.r_0_), channel_id=1, source_target_pairs={{0,16},{1,17},{2,18},{3,19},{4,20},{5,21},{6,22},{7,23},{8,24},{9,... | collective-permute-start | bytes 479240 | tf_op jit(solution)/shard_map/ppermute | solution.py:72
  8.1 12.2 %collective-permute-start.2 = (bf16[104,768]{1,0:T(8,128)(2,1)S(1)}, bf16[104,768]{1,0:T(8,128)(2,1)S(1)}, u32[]{:S(2)}, u32[]{:S(2)}) collective-permute-start(bf16[104,768]{1,0:T(8,128)(2,1)S(1)} %fusion.10.r_0_), channel_id=1, source_target_pairs={{0,24},{1,25},{2,26},{3,27},{4,28},{5,29},{6,30},{7,31},{8,16},{9,... | collective-permute-start | bytes 479240 | tf_op jit(solution)/shard_map/ppermute | solution.py:72
  9.2 20.8 %collective-permute-start.3 = (bf16[192,768]{1,0:T(8,128)(2,1)S(1)}, bf16[192,768]{1,0:T(8,128)(2,1)S(1)}, u32[]{:S(2)}, u32[]{:S(2)}) collective-permute-start(bf16[192,768]{1,0:T(8,128)(2,1)S(1)} %convert_bitcast_fusion.r_4_.r_0_), channel_id=1, source_target_pairs={{0,8},{1,9},{2,10},{3,11},{4,12},{5,13},{6,14},{7,15},{8,0},{9,1},... | collective-permute-start | bytes 884744 | tf_op jit(solution)/shard_map/ppermute | solution.py:72
  10.1 32.5 %collective-permute-start.4 = (bf16[192,768]{1,0:T(8,128)(2,1)S(1)}, bf16[192,768]{1,0:T(8,128)(2,1)S(1)}, u32[]{:S(2)}, u32[]{:S(2)}) collective-permute-start(bf16[192,768]{1,0:T(8,128)(2,1)S(1)} %convert_bitcast_fusion.r_4_.r_0_), channel_id=1, source_target_pairs={{0,16},{1,17},{2,18},{3,19},{4,20},{5,21},{6,22},{7,23},{8,24},{9,... | collective-permute-start | bytes 884744 | tf_op jit(solution)/shard_map/ppermute | solution.py:72
  14.0 28.7 %collective-permute-start.5 = (bf16[192,768]{1,0:T(8,128)(2,1)S(1)}, bf16[192,768]{1,0:T(8,128)(2,1)S(1)}, u32[]{:S(2)}, u32[]{:S(2)}) collective-permute-start(bf16[192,768]{1,0:T(8,128)(2,1)S(1)} %convert_bitcast_fusion.r_4_.r_0_), channel_id=1, source_target_pairs={{0,24},{1,25},{2,26},{3,27},{4,28},{5,29},{6,30},{7,31},{8,16},{9,... | collective-permute-start | bytes 884744 | tf_op jit(solution)/shard_map/ppermute | solution.py:72
  23.6 16.2 %collective-permute-start.6 = (bf16[4,104,768]{2,1,0:T(8,128)(2,1)}, bf16[4,104,768]{2,1,0:T(8,128)(2,1)S(1)}, u32[]{:S(2)}, u32[]{:S(2)}) collective-permute-start(bf16[4,104,768]{2,1,0:T(8,128)(2,1)} %ordered_stack.2.r_0_), channel_id=1, source_target_pairs={{0,2},{1,5},{2,0},{3,7},{4,6},{5,1},{6,4},{7,3},{8,10},{9,13},{10,... | collective-permute-start | bytes 1916936 | tf_op jit(solution)/shard_map/ppermute | solution.py:72
  25.1 21.3 %collective-permute-start.7 = (bf16[4,104,768]{2,1,0:T(8,128)(2,1)}, bf16[4,104,768]{2,1,0:T(8,128)(2,1)S(1)}, u32[]{:S(2)}, u32[]{:S(2)}) collective-permute-start(bf16[4,104,768]{2,1,0:T(8,128)(2,1)} %ordered_stack.2.r_0_), channel_id=1, source_target_pairs={{0,4},{1,3},{2,6},{3,1},{4,0},{5,7},{6,2},{7,5},{8,12},{9,11},{10,... | collective-permute-start | bytes 1916936 | tf_op jit(solution)/shard_map/ppermute | solution.py:72
  30.0 29.0 %collective-permute-start.13 = (bf16[4,256,768]{2,1,0:T(8,128)(2,1)}, bf16[4,256,768]{2,1,0:T(8,128)(2,1)}, u32[]{:S(2)}, u32[]{:S(2)}) collective-permute-start(bf16[4,256,768]{2,1,0:T(8,128)(2,1)} %r_2_.1), channel_id=1, source_target_pairs={{0,1},{1,0},{2,3},{3,2},{4,5},{5,4},{6,7},{7,6},{8,9},{9,8},{10,11... | collective-permute-start | bytes 4718600 | tf_op jit(solution)/shard_map/ppermute | solution.py:72
  41.5 11.4 %collective-permute-start.8 = (bf16[4,104,768]{2,1,0:T(8,128)(2,1)}, bf16[4,104,768]{2,1,0:T(8,128)(2,1)S(1)}, u32[]{:S(2)}, u32[]{:S(2)}) collective-permute-start(bf16[4,104,768]{2,1,0:T(8,128)(2,1)} %gate.6.r_4_.r_5_.r_8_.r_10_), channel_id=1, source_target_pairs={{0,4},{1,3},{2,6},{3,1},{4,0},{5,7},{6,2},{7,5},{8,12},{9,11},{10,... | collective-permute-start | bytes 1916936 | tf_op jit(solution)/shard_map/ppermute | solution.py:72
  47.3 6.6 %collective-permute-start.9 = (bf16[4,104,768]{2,1,0:T(8,128)(2,1)}, bf16[4,104,768]{2,1,0:T(8,128)(2,1)S(1)}, u32[]{:S(2)}, u32[]{:S(2)}) collective-permute-start(bf16[4,104,768]{2,1,0:T(8,128)(2,1)} %gate.7.r_4_.r_7_.r_3_.r_9_), channel_id=1, source_target_pairs={{0,1},{1,0},{2,3},{3,2},{4,5},{5,4},{6,7},{7,6},{8,9},{9,8},{10,11... | collective-permute-start | bytes 1916936 | tf_op jit(solution)/shard_map/ppermute | solution.py:72
  47.8 6.3 %collective-permute-start.10 = (bf16[4,104,768]{2,1,0:T(8,128)(2,1)S(1)}, bf16[4,104,768]{2,1,0:T(8,128)(2,1)S(1)}, u32[]{:S(2)}, u32[]{:S(2)}) collective-permute-start(bf16[4,104,768]{2,1,0:T(8,128)(2,1)S(1)} %copy-done.1), channel_id=1, source_target_pairs={{0,1},{1,0},{2,3},{3,2},{4,5},{5,4},{6,7},{7,6},{8,9},{9,8},{10,11... | collective-permute-start | bytes 1916936 | tf_op jit(solution)/shard_map/ppermute | solution.py:72
  47.8 6.4 %collective-permute-start.11 = (bf16[4,104,768]{2,1,0:T(8,128)(2,1)S(1)}, bf16[4,104,768]{2,1,0:T(8,128)(2,1)S(1)}, u32[]{:S(2)}, u32[]{:S(2)}) collective-permute-start(bf16[4,104,768]{2,1,0:T(8,128)(2,1)S(1)} %collective-permute-done.7.r_6_.r_9_.r_5_.r_11_), channel_id=1, source_target_pairs={{0,1},{1,0},{2,3},{3,2},{4,5},{5,4},{6,7},{7,6},{8,9},{9,8},{10,11... | collective-permute-start | bytes 1916936 | tf_op jit(solution)/shard_map/ppermute | solution.py:72
  52.9 27.5 %collective-permute-start.14 = (bf16[4,192,768]{2,1,0:T(8,128)(2,1)}, bf16[4,192,768]{2,1,0:T(8,128)(2,1)}, u32[]{:S(2)}, u32[]{:S(2)}) collective-permute-start(bf16[4,192,768]{2,1,0:T(8,128)(2,1)} %ordered_stack.3.r_1_.r_7_), channel_id=1, source_target_pairs={{0,2},{1,5},{2,0},{3,7},{4,6},{5,1},{6,4},{7,3},{8,10},{9,13},{10,... | collective-permute-start | bytes 3538952 | tf_op jit(solution)/shard_map/ppermute | solution.py:72
  53.9 29.0 %collective-permute-start.16 = (bf16[4,192,768]{2,1,0:T(8,128)(2,1)}, bf16[4,192,768]{2,1,0:T(8,128)(2,1)}, u32[]{:S(2)}, u32[]{:S(2)}) collective-permute-start(bf16[4,192,768]{2,1,0:T(8,128)(2,1)} %ordered_stack.3.r_1_.r_7_), channel_id=1, source_target_pairs={{0,4},{1,3},{2,6},{3,1},{4,0},{5,7},{6,2},{7,5},{8,12},{9,11},{10,... | collective-permute-start | bytes 3538952 | tf_op jit(solution)/shard_map/ppermute | solution.py:72
  54.1 2.1 collective-permute-start.12
  80.4 16.5 %collective-permute-start.17 = (bf16[4,192,768]{2,1,0:T(8,128)(2,1)}, bf16[4,192,768]{2,1,0:T(8,128)(2,1)S(1)}, u32[]{:S(2)}, u32[]{:S(2)}) collective-permute-start(bf16[4,192,768]{2,1,0:T(8,128)(2,1)} %gate.8.r_20_.r_8_), channel_id=1, source_target_pairs={{0,4},{1,3},{2,6},{3,1},{4,0},{5,7},{6,2},{7,5},{8,12},{9,11},{10,... | collective-permute-start | bytes 3538952 | tf_op jit(solution)/shard_map/ppermute | solution.py:72
  82.5 15.4 %collective-permute-start.15 = (bf16[4,256,768]{2,1,0:T(8,128)(2,1)S(1)}, bf16[4,256,768]{2,1,0:T(8,128)(2,1)S(1)}, u32[]{:S(2)}, u32[]{:S(2)}) collective-permute-start(bf16[4,256,768]{2,1,0:T(8,128)(2,1)S(1)} %copy-done.15), channel_id=1, source_target_pairs={{0,1},{1,0},{2,3},{3,2},{4,5},{5,4},{6,7},{7,6},{8,9},{9,8},{10,11... | collective-permute-start | bytes 4718600 | tf_op jit(solution)/shard_map/ppermute | solution.py:72
  82.5 15.4 %collective-permute-start.18 = (bf16[4,192,768]{2,1,0:T(8,128)(2,1)}, bf16[4,192,768]{2,1,0:T(8,128)(2,1)S(1)}, u32[]{:S(2)}, u32[]{:S(2)}) collective-permute-start(bf16[4,192,768]{2,1,0:T(8,128)(2,1)} %ordered_stack.3.r_1_.r_7_), channel_id=1, source_target_pairs={{0,1},{1,0},{2,3},{3,2},{4,5},{5,4},{6,7},{7,6},{8,9},{9,8},{10,11... | collective-permute-start | bytes 3538952 | tf_op jit(solution)/shard_map/ppermute | solution.py:72
  83.0 14.9 %collective-permute-start.20 = (bf16[4,192,768]{2,1,0:T(8,128)(2,1)}, bf16[4,192,768]{2,1,0:T(8,128)(2,1)S(1)}, u32[]{:S(2)}, u32[]{:S(2)}) collective-permute-start(bf16[4,192,768]{2,1,0:T(8,128)(2,1)} %collective-permute-done.16.r_9_), channel_id=1, source_target_pairs={{0,1},{1,0},{2,3},{3,2},{4,5},{5,4},{6,7},{7,6},{8,9},{9,8},{10,11... | collective-permute-start | bytes 3538952 | tf_op jit(solution)/shard_map/ppermute | solution.py:72
  83.0 15.0 %collective-permute-start.19 = (bf16[4,192,768]{2,1,0:T(8,128)(2,1)}, bf16[4,192,768]{2,1,0:T(8,128)(2,1)S(1)}, u32[]{:S(2)}, u32[]{:S(2)}) collective-permute-start(bf16[4,192,768]{2,1,0:T(8,128)(2,1)} %gate.8.r_20_.r_8_), channel_id=1, source_target_pairs={{0,1},{1,0},{2,3},{3,2},{4,5},{5,4},{6,7},{7,6},{8,9},{9,8},{10,11... | collective-permute-start | bytes 3538952 | tf_op jit(solution)/shard_map/ppermute | solution.py:72
  97.9 3.1 %collective-permute-start.21 = (bf16[4,192,768]{2,1,0:T(8,128)(2,1)}, bf16[4,192,768]{2,1,0:T(8,128)(2,1)S(1)}, u32[]{:S(2)}, u32[]{:S(2)}) collective-permute-start(bf16[4,192,768]{2,1,0:T(8,128)(2,1)} %gate.9.r_10_), channel_id=1, source_target_pairs={{0,1},{1,0},{2,3},{3,2},{4,5},{5,4},{6,7},{7,6},{8,9},{9,8},{10,11... | collective-permute-start | bytes 3538952 | tf_op jit(solution)/shard_map/ppermute | solution.py:72
  149.2 3.1 %collective-permute-start.23 = (bf16[4,192,768]{2,1,0:T(8,128)(2,1)}, bf16[4,192,768]{2,1,0:T(8,128)(2,1)S(1)}, u32[]{:S(2)}, u32[]{:S(2)}) collective-permute-start(bf16[4,192,768]{2,1,0:T(8,128)(2,1)} %get-tuple-element.75), channel_id=1, source_target_pairs={{0,1},{1,0},{2,3},{3,2},{4,5},{5,4},{6,7},{7,6},{8,9},{9,8},{10,11... | collective-permute-start | bytes 3538952 | tf_op jit(solution)/shard_map/ppermute | solution.py:72
  149.4 6.7 %collective-permute-start.24 = (bf16[4,192,768]{2,1,0:T(8,128)(2,1)}, bf16[4,192,768]{2,1,0:T(8,128)(2,1)S(1)}, u32[]{:S(2)}, u32[]{:S(2)}) collective-permute-start(bf16[4,192,768]{2,1,0:T(8,128)(2,1)} %get-tuple-element.77), channel_id=1, source_target_pairs={{0,1},{1,0},{2,3},{3,2},{4,5},{5,4},{6,7},{7,6},{8,9},{9,8},{10,11... | collective-permute-start | bytes 3538952 | tf_op jit(solution)/shard_map/ppermute | solution.py:72
  149.8 28.9 %collective-permute-start.25 = (bf16[4,192,768]{2,1,0:T(8,128)(2,1)}, bf16[4,192,768]{2,1,0:T(8,128)(2,1)S(1)}, u32[]{:S(2)}, u32[]{:S(2)}) collective-permute-start(bf16[4,192,768]{2,1,0:T(8,128)(2,1)} %get-tuple-element.85), channel_id=1, source_target_pairs={{0,1},{1,0},{2,3},{3,2},{4,5},{5,4},{6,7},{7,6},{8,9},{9,8},{10,11... | collective-permute-start | bytes 3538952 | tf_op jit(solution)/shard_map/ppermute | solution.py:72
  154.0 24.7 %collective-permute-start.26 = (bf16[4,192,768]{2,1,0:T(8,128)(2,1)S(1)}, bf16[4,192,768]{2,1,0:T(8,128)(2,1)S(1)}, u32[]{:S(2)}, u32[]{:S(2)}) collective-permute-start(bf16[4,192,768]{2,1,0:T(8,128)(2,1)S(1)} %add_convert_fusion.2.r_11_.r_7_), channel_id=1, source_target_pairs={{0,4},{1,3},{2,6},{3,1},{4,0},{5,7},{6,2},{7,5},{8,12},{9,11},{10,... | collective-permute-start | bytes 3538952 | tf_op jit(solution)/shard_map/ppermute | solution.py:72
  156.1 34.5 %collective-permute-start.27 = (bf16[4,192,768]{2,1,0:T(8,128)(2,1)}, bf16[4,192,768]{2,1,0:T(8,128)(2,1)S(1)}, u32[]{:S(2)}, u32[]{:S(2)}) collective-permute-start(bf16[4,192,768]{2,1,0:T(8,128)(2,1)} %get-tuple-element.91), channel_id=1, source_target_pairs={{0,1},{1,0},{2,3},{3,2},{4,5},{5,4},{6,7},{7,6},{8,9},{9,8},{10,11... | collective-permute-start | bytes 3538952 | tf_op jit(solution)/shard_map/ppermute | solution.py:72
  156.4 34.2 %collective-permute-start.28 = (bf16[4,192,768]{2,1,0:T(8,128)(2,1)S(1)}, bf16[4,192,768]{2,1,0:T(8,128)(2,1)S(1)}, u32[]{:S(2)}, u32[]{:S(2)}) collective-permute-start(bf16[4,192,768]{2,1,0:T(8,128)(2,1)S(1)} %add_convert_fusion.1.r_12_.r_8_), channel_id=1, source_target_pairs={{0,4},{1,3},{2,6},{3,1},{4,0},{5,7},{6,2},{7,5},{8,12},{9,11},{10,... | collective-permute-start | bytes 3538952 | tf_op jit(solution)/shard_map/ppermute | solution.py:72
  180.5 16.3 %collective-permute-start.29 = (bf16[4,192,768]{2,1,0:T(8,128)(2,1)S(1)}, bf16[4,192,768]{2,1,0:T(8,128)(2,1)S(1)}, u32[]{:S(2)}, u32[]{:S(2)}) collective-permute-start(bf16[4,192,768]{2,1,0:T(8,128)(2,1)S(1)} %add_convert_fusion.r_8_), channel_id=1, source_target_pairs={{0,2},{1,5},{2,0},{3,7},{4,6},{5,1},{6,4},{7,3},{8,10},{9,13},{10,... | collective-permute-start | bytes 3538952 | tf_op jit(solution)/shard_map/ppermute | solution.py:72
  199.1 21.8 %collective-permute-start.32 = (bf16[192,768]{1,0:T(8,128)(2,1)S(1)}, bf16[192,768]{1,0:T(8,128)(2,1)S(1)}, u32[]{:S(2)}, u32[]{:S(2)}) collective-permute-start(bf16[192,768]{1,0:T(8,128)(2,1)S(1)} %get-tuple-element.132.r_18_), channel_id=1, source_target_pairs={{0,16},{1,17},{2,18},{3,19},{4,20},{5,21},{6,22},{7,23},{8,24},{9,... | collective-permute-start | bytes 884744 | tf_op jit(solution)/shard_map/ppermute | solution.py:72
  221.6 5.7 %collective-permute-start.38 = (bf16[4,104,768]{2,1,0:T(8,128)(2,1)}, bf16[4,104,768]{2,1,0:T(8,128)(2,1)}, u32[]{:S(2)}, u32[]{:S(2)}) collective-permute-start(bf16[4,104,768]{2,1,0:T(8,128)(2,1)} %gate.11), channel_id=1, source_target_pairs={{0,1},{1,0},{2,3},{3,2},{4,5},{5,4},{6,7},{7,6},{8,9},{9,8},{10,11... | collective-permute-start | bytes 1916936 | tf_op jit(solution)/shard_map/ppermute | solution.py:72
  221.6 8.3 %collective-permute-start.22 = (bf16[2,256,768]{2,1,0:T(8,128)(2,1)}, bf16[2,256,768]{2,1,0:T(8,128)(2,1)}, u32[]{:S(2)}, u32[]{:S(2)}) collective-permute-start(bf16[2,256,768]{2,1,0:T(8,128)(2,1)} %get-tuple-element.70), channel_id=1, source_target_pairs={{0,1},{1,0},{2,3},{3,2},{4,5},{5,4},{6,7},{7,6},{8,9},{9,8},{10,11... | collective-permute-start | bytes 2359304 | tf_op jit(solution)/shard_map/ppermute | solution.py:72
  226.6 6.9 %collective-permute-start.35 = (bf16[4,104,768]{2,1,0:T(8,128)(2,1)}, bf16[4,104,768]{2,1,0:T(8,128)(2,1)S(1)}, u32[]{:S(2)}, u32[]{:S(2)}) collective-permute-start(bf16[4,104,768]{2,1,0:T(8,128)(2,1)} %get-tuple-element.97), channel_id=1, source_target_pairs={{0,1},{1,0},{2,3},{3,2},{4,5},{5,4},{6,7},{7,6},{8,9},{9,8},{10,11... | collective-permute-start | bytes 1916936 | tf_op jit(solution)/shard_map/ppermute | solution.py:72
  226.7 9.9 %collective-permute-start.37 = (bf16[4,104,768]{2,1,0:T(8,128)(2,1)}, bf16[4,104,768]{2,1,0:T(8,128)(2,1)S(1)}, u32[]{:S(2)}, u32[]{:S(2)}) collective-permute-start(bf16[4,104,768]{2,1,0:T(8,128)(2,1)} %get-tuple-element.99), channel_id=1, source_target_pairs={{0,1},{1,0},{2,3},{3,2},{4,5},{5,4},{6,7},{7,6},{8,9},{9,8},{10,11... | collective-permute-start | bytes 1916936 | tf_op jit(solution)/shard_map/ppermute | solution.py:72
  227.2 24.6 %collective-permute-start.30 = (f32[2,256,768]{2,1,0:T(8,128)}, f32[2,256,768]{2,1,0:T(8,128)S(1)}, u32[]{:S(2)}, u32[]{:S(2)}) collective-permute-start(f32[2,256,768]{2,1,0:T(8,128)} %get-tuple-element.93), channel_id=1, source_target_pairs={{0,1},{1,0},{2,3},{3,2},{4,5},{5,4},{6,7},{7,6},{8,9},{9,8},{10,11... | collective-permute-start | bytes 4718600 | tf_op jit(solution)/shard_map/ppermute | solution.py:72
  228.8 10.5 %collective-permute-start.39 = (bf16[4,104,768]{2,1,0:T(8,128)(2,1)S(1)}, bf16[4,104,768]{2,1,0:T(8,128)(2,1)S(1)}, u32[]{:S(2)}, u32[]{:S(2)}) collective-permute-start(bf16[4,104,768]{2,1,0:T(8,128)(2,1)S(1)} %add_convert_fusion.4), channel_id=1, source_target_pairs={{0,4},{1,3},{2,6},{3,1},{4,0},{5,7},{6,2},{7,5},{8,12},{9,11},{10,... | collective-permute-start | bytes 1916936 | tf_op jit(solution)/shard_map/ppermute | solution.py:72
  233.5 9.9 %collective-permute-start.31 = (bf16[192,768]{1,0:T(8,128)(2,1)S(1)}, bf16[192,768]{1,0:T(8,128)(2,1)S(1)}, u32[]{:S(2)}, u32[]{:S(2)}) collective-permute-start(bf16[192,768]{1,0:T(8,128)(2,1)S(1)} %copy-done.27), channel_id=1, source_target_pairs={{0,8},{1,9},{2,10},{3,11},{4,12},{5,13},{6,14},{7,15},{8,0},{9,1},... | collective-permute-start | bytes 884744 | tf_op jit(solution)/shard_map/ppermute | solution.py:72
  233.5 15.3 %collective-permute-start.33 = (bf16[192,768]{1,0:T(8,128)(2,1)S(1)}, bf16[192,768]{1,0:T(8,128)(2,1)S(1)}, u32[]{:S(2)}, u32[]{:S(2)}) collective-permute-start(bf16[192,768]{1,0:T(8,128)(2,1)S(1)} %copy-done.26), channel_id=1, source_target_pairs={{0,24},{1,25},{2,26},{3,27},{4,28},{5,29},{6,30},{7,31},{8,16},{9,... | collective-permute-start | bytes 884744 | tf_op jit(solution)/shard_map/ppermute | solution.py:72
  236.6 16.1 %collective-permute-start.34 = (bf16[4,104,768]{2,1,0:T(8,128)(2,1)}, bf16[4,104,768]{2,1,0:T(8,128)(2,1)}, u32[]{:S(2)}, u32[]{:S(2)}) collective-permute-start(bf16[4,104,768]{2,1,0:T(8,128)(2,1)} %get-tuple-element.95), channel_id=1, source_target_pairs={{0,1},{1,0},{2,3},{3,2},{4,5},{5,4},{6,7},{7,6},{8,9},{9,8},{10,11... | collective-permute-start | bytes 1916936 | tf_op jit(solution)/shard_map/ppermute | solution.py:72
  239.3 16.4 %collective-permute-start.36 = (bf16[4,104,768]{2,1,0:T(8,128)(2,1)}, bf16[4,104,768]{2,1,0:T(8,128)(2,1)}, u32[]{:S(2)}, u32[]{:S(2)}) collective-permute-start(bf16[4,104,768]{2,1,0:T(8,128)(2,1)} %add_convert_fusion.5), channel_id=1, source_target_pairs={{0,4},{1,3},{2,6},{3,1},{4,0},{5,7},{6,2},{7,5},{8,12},{9,11},{10,... | collective-permute-start | bytes 1916936 | tf_op jit(solution)/shard_map/ppermute | solution.py:72
  243.4 12.3 %collective-permute-start.40 = (bf16[4,104,768]{2,1,0:T(8,128)(2,1)S(1)}, bf16[4,104,768]{2,1,0:T(8,128)(2,1)S(1)}, u32[]{:S(2)}, u32[]{:S(2)}) collective-permute-start(bf16[4,104,768]{2,1,0:T(8,128)(2,1)S(1)} %add_convert_fusion.3), channel_id=1, source_target_pairs={{0,2},{1,5},{2,0},{3,7},{4,6},{5,1},{6,4},{7,3},{8,10},{9,13},{10,... | collective-permute-start | bytes 1916936 | tf_op jit(solution)/shard_map/ppermute | solution.py:72
  257.2 9.5 %collective-permute-start.41 = (bf16[104,768]{1,0:T(8,128)(2,1)S(1)}, bf16[104,768]{1,0:T(8,128)(2,1)S(1)}, u32[]{:S(2)}, u32[]{:S(2)}) collective-permute-start(bf16[104,768]{1,0:T(8,128)(2,1)S(1)} %get-tuple-element.134), channel_id=1, source_target_pairs={{0,8},{1,9},{2,10},{3,11},{4,12},{5,13},{6,14},{7,15},{8,0},{9,1},... | collective-permute-start | bytes 479240 | tf_op jit(solution)/shard_map/ppermute | solution.py:72
  257.3 14.8 %collective-permute-start.42 = (bf16[104,768]{1,0:T(8,128)(2,1)S(1)}, bf16[104,768]{1,0:T(8,128)(2,1)S(1)}, u32[]{:S(2)}, u32[]{:S(2)}) collective-permute-start(bf16[104,768]{1,0:T(8,128)(2,1)S(1)} %get-tuple-element.136), channel_id=1, source_target_pairs={{0,16},{1,17},{2,18},{3,19},{4,20},{5,21},{6,22},{7,23},{8,24},{9,... | collective-permute-start | bytes 479240 | tf_op jit(solution)/shard_map/ppermute | solution.py:72
  258.5 14.8 %copy-start.21 = (f32[768,96]{0,1:T(8,128)S(1)}, f32[768,96]{0,1:T(8,128)}, u32[]{:S(2)}) copy-start(f32[768,96]{0,1:T(8,128)} %param.17) | copy-start | bytes 884740
  258.5 14.8 %copy-start.34 = (f32[768,96]{0,1:T(8,128)S(1)}, f32[768,96]{0,1:T(8,128)}, u32[]{:S(2)}) copy-start(f32[768,96]{0,1:T(8,128)} %param.19) | copy-start | bytes 884740
  258.5 14.8 %copy-start.35 = (f32[768,96]{0,1:T(8,128)S(1)}, f32[768,96]{0,1:T(8,128)}, u32[]{:S(2)}) copy-start(f32[768,96]{0,1:T(8,128)} %param.18) | copy-start | bytes 884740
  258.5 13.6 %collective-permute-start.43 = (bf16[104,768]{1,0:T(8,128)(2,1)S(1)}, bf16[104,768]{1,0:T(8,128)(2,1)S(1)}, u32[]{:S(2)}, u32[]{:S(2)}) collective-permute-start(bf16[104,768]{1,0:T(8,128)(2,1)S(1)} %get-tuple-element.135), channel_id=1, source_target_pairs={{0,24},{1,25},{2,26},{3,27},{4,28},{5,29},{6,30},{7,31},{8,16},{9,... | collective-permute-start | bytes 479240 | tf_op jit(solution)/shard_map/ppermute | solution.py:72
  (42 other events, 188.3 us)
where the time goes:
time: 280 us; the launch traced here: 275 us
  Pallas kernels  131 us (47%)
  waiting for transfers between devices  57.9 us (21%)
  starting transfers between devices  40.8 us (15%)
  other arithmetic  22.2 us (8%)
  local copies, waits for them, and re-layouts  17.8 us (6%)
  between operations  5.52 us (2%)
    ppermute x44, waiting for transfers between devices, permute(): return lax.ppermute(value, AXES, pairs)  57.9 us
    pallas_call x1, Pallas kernels, ffn_call(): pl.pallas_call(lambda *r: ffn_kernel(grid, per, *r), in_specs=[SMEM, VMEM...  47.2 us
    ppermute x44, starting transfers between devices, permute(): return lax.ppermute(value, AXES, pairs)  40.8 us
    pallas_call x2, Pallas kernels, attend_back_call(): pl.pallas_call(lambda *r: attend_back_kernel(seq, *r), grid=(pairs,), in_...  22.8 us
    pallas_call x2, Pallas kernels, attend_call(): pl.pallas_call(lambda *r: attend_kernel(grid, len(pieces), seq, *r), grid...  22.5 us
    pallas_call x1, Pallas kernels, attn_grad_call(): pl.pallas_call(lambda *r: attn_grad_kernel(grid, per, len(pieces), *r), i...  17.4 us
    pallas_call x1, Pallas kernels, qkv_call(): pl.pallas_call(lambda *r: qkv_kernel(grid, *r), in_specs=[SMEM, VMEM, ANY...  9.24 us
    unnamed x99, local copies, waits for them, and re-layouts  7.92 us
  transfers between devices with their start and end apart: 44, of which 15 were waited for; matrix products, arithmetic and copies ran while one was open for 9% of the time, Pallas kernels for 30%

commit v1 on v0

--- a/solution.py
+++ b/solution.py
@@ -843,13 +843,10 @@
 
 
 def attn_grad_kernel(
-    grid, per, npieces, me_ref, sums, db1, db_a, db_b, dz_hbm, x_hbm, gout_hbm, dres_hbm, *rest
+    grid, per, me_ref, sums, db1, db_a, db_b, dz_hbm, x_hbm, gout_hbm, *rest
 ):
-    pieces = rest[:npieces]
     count = 8 if is_path(grid, per) else 2
-    grads, (mine, others) = rest[-13 - count : -13], rest[-13:-11]
-    stage, dz, x, gout, line, total, w = rest[-11:-4]
-    isem, osem, wsem, dsem = rest[-4:]
+    grads, (stage, dz, x, gout, line, isem, osem) = rest[-7 - count : -7], rest[-7:]
     rows, width = x.shape
     me = me_ref[0]
     core = me & 1
@@ -860,9 +857,6 @@
     loads += [pltpu.make_async_copy(dz_hbm.at[p], dz.at[p], isem.at[p]) for p in range(3)]
     for copy in loads:
         copy.start()
-    load_total = pltpu.make_async_copy(dres_hbm, total, isem.at[5])
-    load_total.start()
-    start_natural(grid, me_ref, pieces, w, wsem, 0, 3 * blocks)
 
     db = db_a[...] + db_b[...]
     tail = 3 * width + FF
@@ -907,46 +901,95 @@
     for part in range(3):
         loads[2 + part].wait()
         emit(part, tn(dz[part], x[...]))
-    load_total.wait()
-    for part in range(3):
-        wait_natural(grid, pieces, w, wsem, part * blocks, blocks, 0, 3 * blocks)
-        total[...] += nn(dz[part], w[part * width : (part + 1) * width, :])
-    for copy in store_sequences(me_ref, total, mine, others, dsem) + copies:
+    for copy in copies:
         copy.wait()
 
 
-def attn_grad_call(grid, me, dz, x, gout, dres, vectors, pieces, per, shape, deps):
+def attn_grad_call(grid, me, dz, x, gout, vectors, per, deps):
     rows, width = x.shape
     paths = path_shapes(grid, grid.devices, per, width)
     path = is_path(grid, per)
     if path:
         paths = [jax.ShapeDtypeStruct((p.shape[0], per + 8, width), BF) for p in paths]
     return pl.pallas_call(
-        lambda *r: attn_grad_kernel(grid, per, len(pieces), *r),
-        in_specs=[SMEM] + [VMEM] * len(vectors) + [ANY] * (4 + len(pieces) + len(deps)),
-        out_specs=[ANY if path else VMEM] * len(paths) + [ANY, ANY],
-        out_shape=paths
-        + [
-            jax.ShapeDtypeStruct(shape, F32),
-            jax.ShapeDtypeStruct((shape[0] // 2,) + shape[1:], F32),
-        ],
+        lambda *r: attn_grad_kernel(grid, per, *r),
+        in_specs=[SMEM] + [VMEM] * len(vectors) + [ANY] * (3 + len(deps)),
+        out_specs=[ANY if path else VMEM] * len(paths),
+        out_shape=paths,
         scratch_shapes=[
             pltpu.VMEM((grid.devices, per + 8, width), BF),
             pltpu.VMEM((3, rows, width), BF),
             pltpu.VMEM((rows, width), BF),
             pltpu.VMEM((width, width), BF),
             pltpu.VMEM((1, 8 * width + FF), F32),
-            pltpu.VMEM((rows, width), F32),
-            pltpu.VMEM((3 * width, width), BF),
-            pltpu.SemaphoreType.DMA((6,)),
+            pltpu.SemaphoreType.DMA((5,)),
             pltpu.SemaphoreType.DMA((grid.devices,)),
-            pltpu.SemaphoreType.DMA((grid.devices,)),
-            pltpu.SemaphoreType.DMA((shape[0],)),
         ],
         compiler_params=params(),
         cost_estimate=cost(6 * rows * width * width, 28 << 20),
         name="attn_grad",
-    )(me, *vectors, dz, x, gout, dres, *pieces, *deps)
+    )(me, *vectors, dz, x, gout, *deps)
+
+
+def input_grad_kernel(grid, npieces, me_ref, dz_hbm, dres_hbm, *rest):
+    pieces = rest[:npieces]
+    mine, others, _, dz, total, w, sems, isem, osem = rest[-9:]
+    rows, width = total.shape
+    blocks = grid.devices // 4
+
+    def load(part):
+        return pltpu.make_async_copy(dz_hbm.at[part], dz.at[part], isem.at[part])
+
+    def in_order(body):
+        for i in range(4):
+            part = quarter_order(grid, me_ref, pieces, i)
+            pl.when(part < 3)(lambda part=part: body(part))
+
+    load_total = pltpu.make_async_copy(dres_hbm, total, isem.at[3])
+    load_total.start()
+    in_order(lambda part: load(part).start())
+    start_natural(grid, me_ref, pieces, w, sems, 0, 3 * blocks)
+    load_total.wait()
+
+    @pl.loop(0, 4)
+    def _(i):
+        part = quarter_order(grid, me_ref, pieces, i)
+
+        @pl.when(part < 3)
+        def _():
+            load(part).wait()
+            wait_natural(grid, pieces, w, sems, part * blocks, blocks, 0, 3 * blocks)
+            at = pl.ds(pl.multiple_of(part * width, width), width)
+            total[...] += nn(dz[part], w[at, :])
+
+    for copy in store_sequences(me_ref, total, mine, others, osem):
+        copy.wait()
+
+
+def input_grad_call(grid, me, dz, dres, pieces, shape, carry, deps):
+    rows, width = dres.shape
+    return pl.pallas_call(
+        lambda *r: input_grad_kernel(grid, len(pieces), *r),
+        in_specs=[SMEM, ANY, ANY] + [ANY] * (len(pieces) + 1 + len(deps)),
+        out_specs=[ANY, ANY, ANY],
+        out_shape=[
+            jax.ShapeDtypeStruct(shape, F32),
+            jax.ShapeDtypeStruct((shape[0] // 2,) + shape[1:], F32),
+            jax.ShapeDtypeStruct(carry.shape, carry.dtype),
+        ],
+        input_output_aliases={3 + len(pieces): 2},
+        scratch_shapes=[
+            pltpu.VMEM((3, rows, width), BF),
+            pltpu.VMEM((rows, width), F32),
+            pltpu.VMEM((3 * width, width), BF),
+            pltpu.SemaphoreType.DMA((grid.devices,)),
+            pltpu.SemaphoreType.DMA((4,)),
+            pltpu.SemaphoreType.DMA((shape[0],)),
+        ],
+        compiler_params=params(),
+        cost_estimate=cost(3 * rows * width * width, 16 << 20),
+        name="input_grad",
+    )(me, dz, dres, *pieces, carry, *deps)
 
 
 def gate(value, deps):
@@ -1092,13 +1135,16 @@
         lens, qkv, dctx, lse, seqs, 1, dz, sums_f.keep[0], sends
     )
     sends = sums_f.add_two()
-    *grads_c, dx, dx_other = attn_grad_call(
-        grid, me, dz, x, gout, dres_one, [sums, db1, db_a, db_b], weights, per, tokens.shape, sends
+    grads_c = list(
+        attn_grad_call(grid, me, dz, x, gout, [sums, db1, db_a, db_b], per, sends)
     )
     if path:
         grads_c[7] = gate(grads_c[7], sums_f.z[1:2])
     sums_c = Sums(grid, path, grads_c)
-    sums_c.add_core()
+    sends = sums_c.add_core()
+    dx, dx_other, sums_c.keep[1] = input_grad_call(
+        grid, me, dz, dres_one, weights, tokens.shape, sums_c.keep[1], sends
+    )
     ffn_sum = sums_f.add_z()
     sums_c.add_three()
     sums_c.keep[0] = gate(sums_c.keep[0], [ffn_sum])

time: 280 us -> 280 us (level)
  waiting for transfers between devices: 57.9 us -> 53 us
  other arithmetic: 22.2 us -> 25.8 us
  Pallas kernels: 131 us -> 134 us
    ppermute x44, waiting for transfers between devices: 57.9 us -> 53 us  [permute(): return lax.ppermute(value, AXES, pairs)]
    pallas_call x1 -> x2, Pallas kernels: 17.4 us -> 20.1 us  [the longest x1 10.6 us: input_grad_call(): pl.pallas_call(lambda *r: input_grad_kernel(grid, len(pieces), *r), in_sp...]
    unnamed x99 -> x101, local copies, waits for them, and re-layouts: 7.92 us -> 7.93 us
  transfers between devices with their start and end apart: 44 -> 44, of which waited for: 15 -> 15; matrix products, arithmetic and copies ran while one was open for 9% -> 11% of each run, Pallas kernels for 30% -> 32%
where the time goes in v1:
time: 280 us; the launch traced here: 276 us
  Pallas kernels  134 us (48%)
  waiting for transfers between devices  53 us (19%)
  starting transfers between devices  39.5 us (14%)
  other arithmetic  25.8 us (9%)
  local copies, waits for them, and re-layouts  17.5 us (6%)
  between operations  5.49 us (2%)
    ppermute x44, waiting for transfers between devices, permute(): return lax.ppermute(value, AXES, pairs)  53 us
    pallas_call x1, Pallas kernels, ffn_call(): pl.pallas_call(lambda *r: ffn_kernel(grid, per, *r), in_specs=[SMEM, VMEM...  47 us
    ppermute x44, starting transfers between devices, permute(): return lax.ppermute(value, AXES, pairs)  39.5 us
    pallas_call x2, Pallas kernels, attend_back_call(): pl.pallas_call(lambda *r: attend_back_kernel(seq, *r), grid=(pairs,), in_...  22.9 us
    pallas_call x2, Pallas kernels, attend_call(): pl.pallas_call(lambda *r: attend_kernel(grid, len(pieces), seq, *r), grid...  22.8 us
    pallas_call x1, Pallas kernels, input_grad_call(): pl.pallas_call(lambda *r: input_grad_kernel(grid, len(pieces), *r), in_sp...  10.6 us
    pallas_call x1, Pallas kernels, attn_grad_call(): pl.pallas_call(lambda *r: attn_grad_kernel(grid, per, *r), in_specs=[SMEM...  9.52 us
    pallas_call x1, Pallas kernels, qkv_call(): pl.pallas_call(lambda *r: qkv_kernel(grid, *r), in_specs=[SMEM, VMEM, ANY...  9.32 us
  transfers between devices with their start and end apart: 44, of which 15 were waited for; matrix products, arithmetic and copies ran while one was open for 11% of the time, Pallas kernels for 32%

profile of v1, /device:TPU:0, one launch (start us, length us, event | category | flops | bytes accessed | tf_op | source)
XLA Modules:
  0.0 275.6 jit_solution(6511845582125748755)
XLA Ops:
  2.4 3.1 %collective-permute-start = (bf16[104,768]{1,0:T(8,128)(2,1)S(1)}, bf16[104,768]{1,0:T(8,128)(2,1)S(1)}, u32[]{:S(2)}, u32[]{:S(2)}) collective-permute-start(bf16[104,768]{1,0:T(8,128)(2,1)S(1)} %fusion.10.r_0_), channel_id=1, source_target_pairs={{0,8},{1,9},{2,10},{3,11},{4,12},{5,13},{6,14},{7,15},{8,0},{9,1},... | collective-permute-start | bytes 479240 | tf_op jit(solution)/shard_map/ppermute | solution.py:72
  5.5 2.6 collective-permute-start.1
  10.1 3.5 %collective-permute-start.4 = (bf16[192,768]{1,0:T(8,128)(2,1)S(1)}, bf16[192,768]{1,0:T(8,128)(2,1)S(1)}, u32[]{:S(2)}, u32[]{:S(2)}) collective-permute-start(bf16[192,768]{1,0:T(8,128)(2,1)S(1)} %convert_bitcast_fusion.r_4_.r_0_), channel_id=1, source_target_pairs={{0,16},{1,17},{2,18},{3,19},{4,20},{5,21},{6,22},{7,23},{8,24},{9,... | collective-permute-start | bytes 884744 | tf_op jit(solution)/shard_map/ppermute | solution.py:72
  14.0 3.1 %collective-permute-start.5 = (bf16[192,768]{1,0:T(8,128)(2,1)S(1)}, bf16[192,768]{1,0:T(8,128)(2,1)S(1)}, u32[]{:S(2)}, u32[]{:S(2)}) collective-permute-start(bf16[192,768]{1,0:T(8,128)(2,1)S(1)} %convert_bitcast_fusion.r_4_.r_0_), channel_id=1, source_target_pairs={{0,24},{1,25},{2,26},{3,27},{4,28},{5,29},{6,30},{7,31},{8,16},{9,... | collective-permute-start | bytes 884744 | tf_op jit(solution)/shard_map/ppermute | solution.py:72
  17.1 3.2 %collective-permute-done.1.r_2_ = bf16[104,768]{1,0:T(8,128)(2,1)S(1)} collective-permute-done((bf16[104,768]{1,0:T(8,128)(2,1)S(1)}, bf16[104,768]{1,0:T(8,128)(2,1)S(1)}, u32[]{:S(2)}, u32[]{:S(2)}) %collective-permute-start.1) | collective-permute-done | bytes 159776 | tf_op jit(solution)/shard_map/ppermute | solution.py:72
  21.6 2.0 ordered_stack.2.r_0_
  23.7 1.5 collective-permute-start.6
  25.1 1.5 collective-permute-start.7
  27.4 1.4 broadcast_select_fusion.3
  30.0 9.8 %collective-permute-done.6.r_0_ = bf16[4,104,768]{2,1,0:T(8,128)(2,1)S(1)} collective-permute-done((bf16[4,104,768]{2,1,0:T(8,128)(2,1)}, bf16[4,104,768]{2,1,0:T(8,128)(2,1)S(1)}, u32[]{:S(2)}, u32[]{:S(2)}) %collective-permute-start.6) | collective-permute-done | bytes 639008 | tf_op jit(solution)/shard_map/ppermute | solution.py:72
  41.5 1.2 collective-permute-done.4.r_2_
  44.1 2.4 ordered_stack.3.r_1_.r_7_
  48.3 4.5 %collective-permute-done.8.r_7_.r_10_.r_6_ = bf16[4,104,768]{2,1,0:T(8,128)(2,1)S(1)} collective-permute-done((bf16[4,104,768]{2,1,0:T(8,128)(2,1)}, bf16[4,104,768]{2,1,0:T(8,128)(2,1)S(1)}, u32[]{:S(2)}, u32[]{:S(2)}) %collective-permute-start.8) | collective-permute-done | bytes 639008 | tf_op jit(solution)/shard_map/ppermute | solution.py:72
  54.2 2.0 collective-permute-done.12.r_11_.r_14_.r_10_
  58.8 9.3 %qkv.1 = (bf16[1024,2304]{1,0:T(8,128)(2,1)}, bf16[1024,768]{1,0:T(8,128)(2,1)}) custom-call(s32[3]{0:T(128)} %pad_add_fusion.1.r_0_.r_1_, f32[1,9216]{1,0:T(1,128)} %reshape.78.r_1_.r_6_, bf16[4,256,768]{2,1,0:T(8,128)(2,1)} %r_2_.1, bf16[4,256,768]{2,1,0:T(8,128)(2,1)} %collective-permute-done.13.r_3_, bf16[4,104,768]{2,1,0:T(8,128)(2,1)} %gate.7.r_4_.r_7_.r_3_, ...), custom_call_target="tpu_custom_call" | custom-call | flops 226492416 | bytes 786432 | tf_op jit(solution)/shard_map/qkv/pallas_call | solution.py:399
  68.1 12.1 %attend.2 = (bf16[1024,768]{1,0:T(8,128)(2,1)}, f32[12,2,512]{2,1,0:T(2,128)}, f32[1024,768]{1,0:T(8,128)}, f32[1024,1]{1,0:T(8,128)}, bf16[1024,768]{1,0:T(8,128)(2,1)}) custom-call(s32[2]{0:T(128)} %fusion.19.r_0_, s32[3]{0:T(128)} %pad_add_fusion.1.r_0_.r_1_, bf16[1024,2304]{1,0:T(8,128)(2,1)} %get-tuple-element.59.r_2_.r_3_.r_4_.r_1_, ...), custom_call_target="tpu_custom_call" | custom-call | flops 201326592 | bytes 589824 | tf_op jit(solution)/shard_map/attend/pallas_call | solution.py:488
  80.2 2.1 collective-permute-start.17
  83.3 10.7 %attend.3 = (bf16[1024,768]{1,0:T(8,128)(2,1)}, f32[12,2,512]{2,1,0:T(2,128)}, f32[1024,768]{1,0:T(8,128)}, f32[1024,1]{1,0:T(8,128)}, bf16[1024,768]{1,0:T(8,128)(2,1)}) custom-call(s32[2]{0:T(128)} %fusion.19.r_0_, s32[3]{0:T(128)} %pad_add_fusion.1.r_0_.r_1_, ...), custom_call_target="tpu_custom_call", output_to_operand_aliasing={{0}: (15, {}), {1}: (16, {}), {2}: (17, {}), {3}: (18, {}),... | custom-call | flops 201326592 | bytes 589824 | tf_op jit(solution)/shard_map/attend/pallas_call | solution.py:488
  94.1 2.6 collective-permute-done.17.r_0_
  97.8 3.0 %collective-permute-done.21.r_14_ = bf16[4,192,768]{2,1,0:T(8,128)(2,1)S(1)} collective-permute-done((bf16[4,192,768]{2,1,0:T(8,128)(2,1)}, bf16[4,192,768]{2,1,0:T(8,128)(2,1)S(1)}, u32[]{:S(2)}, u32[]{:S(2)}) %collective-permute-start.21) | collective-permute-done | bytes 1179680 | tf_op jit(solution)/shard_map/ppermute | solution.py:72
  101.8 47.0 %ffn.1 = (bf16[4,256,768]{2,1,0:T(8,128)(2,1)}, bf16[2,256,768]{2,1,0:T(8,128)(2,1)}, f32[1024,768]{1,0:T(8,128)}, bf16[1024,768]{1,0:T(8,128)(2,1)}, f32[8,768]...) custom-call(s32[3]{0:T(128)} %pad_add_fusion.1.r_0_.r_1_, ...), custom_call_target="tpu_custom_call" | custom-call | flops 1811939328 | bytes 2621440 | tf_op jit(solution)/shard_map/ffn/pallas_call | solution.py:681
  149.6 2.4 collective-permute-done.23
  152.0 1.7 add_convert_fusion.2.r_11_.r_7_
  153.7 2.1 collective-permute-start.26
  157.1 7.5 %out_back.1 = (bf16[1024,768]{1,0:T(8,128)(2,1)}, bf16[768,768]{1,0:T(8,128)(2,1)}) custom-call(s32[3]{0:T(128)} %pad_add_fusion.1.r_0_.r_1_, bf16[1024,768]{1,0:T(8,128)(2,1)} %get-tuple-element.72.r_1_, bf16[1024,768]{1,0:T(8,128)(2,1)} %get-tuple-element.69.r_1_.r_2_, bf16[4,104,768]{2,1,0:T(8,128)(2,1)} %gate.7.r_4_.r_7_.r_3_, ...), custom_call_target="tpu_custom_call" | custom-call | flops 150994944 | bytes 786432 | tf_op jit(solution)/shard_map/out_back/pallas_call | solution.py:746
  164.6 13.9 %attend_back.2 = (bf16[3,1024,768]{2,1,0:T(8,128)(2,1)}, f32[2,768]{1,0:T(2,128)}, bf16[4,192,768]{2,1,0:T(8,128)(2,1)}) custom-call(s32[2]{0:T(128)} %fusion.19.r_0_, bf16[1024,2304]{1,0:T(8,128)(2,1)} %get-tuple-element.59.r_2_.r_3_.r_4_.r_1_, bf16[1024,2304]{1,0:T(8,128)(2,1)} %get-tuple-element.59.r_2_.r_3_.r_4_.r_1_, ...), custom_call_target="tpu_custom_call", output_to_operand_aliasing={{2}: (6, {})} | custom-call | flops 503316480 | bytes 393216 | tf_op jit(solution)/shard_map/attend_back/pallas_call | solution.py:814
  178.6 1.7 add_convert_fusion.r_8_
  181.4 9.0 %attend_back.3 = (bf16[3,1024,768]{2,1,0:T(8,128)(2,1)}, f32[2,768]{1,0:T(2,128)}, bf16[4,192,768]{2,1,0:T(8,128)(2,1)}) custom-call(s32[2]{0:T(128)} %fusion.19.r_0_, bf16[1024,2304]{1,0:T(8,128)(2,1)} %get-tuple-element.59.r_2_.r_3_.r_4_.r_1_, ...), custom_call_target="tpu_custom_call", output_to_operand_aliasing={{2}: (6, {}), {0}: (7, {})} | custom-call | flops 503316480 | bytes 393216 | tf_op jit(solution)/shard_map/attend_back/pallas_call | solution.py:814
  190.4 6.2 %collective-permute-done.29 = bf16[4,192,768]{2,1,0:T(8,128)(2,1)S(1)} collective-permute-done((bf16[4,192,768]{2,1,0:T(8,128)(2,1)S(1)}, bf16[4,192,768]{2,1,0:T(8,128)(2,1)S(1)}, u32[]{:S(2)}, u32[]{:S(2)}) %collective-permute-start.29) | collective-permute-done | bytes 1179680 | tf_op jit(solution)/shard_map/ppermute | solution.py:72
  196.6 2.8 %fusion.9 = (bf16[192,768]{1,0:T(8,128)(2,1)}, bf16[192,768]{1,0:T(8,128)(2,1)S(1)}, bf16[192,768]{1,0:T(8,128)(2,1)}) fusion(bf16[4,192,768]{2,1,0:T(8,128)(2,1)S(1)} %collective-permute-done.29, bf16[4,192,768]{2,1,0:T(8,128)(2,1)S(1)} %collective-permute-done.28, bf16[4,192,768]{2,1,0:T(8,128)(2,1)S(1)} %collective-permute-done.27, ...), kind=kLoop, calls=%fused_computation.33 | loop fusion | flops 3538944 | bytes 4423680 | tf_op jit(solution)/shard_map/convert_element_type | solution.py:259
  199.4 4.5 %collective-permute-start.30 = (bf16[192,768]{1,0:T(8,128)(2,1)S(1)}, bf16[192,768]{1,0:T(8,128)(2,1)S(1)}, u32[]{:S(2)}, u32[]{:S(2)}) collective-permute-start(bf16[192,768]{1,0:T(8,128)(2,1)S(1)} %get-tuple-element.134.r_9_), channel_id=1, source_target_pairs={{0,16},{1,17},{2,18},{3,19},{4,20},{5,21},{6,22},{7,23},{8,24},{9,... | collective-permute-start | bytes 884744 | tf_op jit(solution)/shard_map/ppermute | solution.py:72
  203.9 9.5 %attn_grad.1 = (bf16[4,104,768]{2,1,0:T(8,128)(2,1)}, bf16[4,104,768]{2,1,0:T(8,128)(2,1)}, bf16[4,104,768]{2,1,0:T(8,128)(2,1)}, bf16[4,104,768]{2,1,0:T(8,128)...) custom-call(s32[3]{0:T(128)} %pad_add_fusion.1.r_0_.r_1_, ...), custom_call_target="tpu_custom_call" | custom-call | flops 452984832 | bytes 1835008 | tf_op jit(solution)/shard_map/attn_grad/pallas_call | solution.py:914
  213.4 3.6 %collective-permute-done.30.r_1_ = bf16[192,768]{1,0:T(8,128)(2,1)S(1)} collective-permute-done((bf16[192,768]{1,0:T(8,128)(2,1)S(1)}, bf16[192,768]{1,0:T(8,128)(2,1)S(1)}, u32[]{:S(2)}, u32[]{:S(2)}) %collective-permute-start.30) | collective-permute-done | bytes 294944 | tf_op jit(solution)/shard_map/ppermute | solution.py:72
  218.4 1.9 collective-permute-done.31
  220.4 1.1 collective-permute-start.39
  223.1 2.1 add_convert_fusion.4.r_13_
  225.2 10.6 %input_grad.1 = (f32[4,256,768]{2,1,0:T(8,128)}, f32[2,256,768]{2,1,0:T(8,128)}, bf16[4,104,768]{2,1,0:T(8,128)(2,1)}) custom-call(s32[3]{0:T(128)} %pad_add_fusion.1.r_0_.r_1_, bf16[3,1024,768]{2,1,0:T(8,128)(2,1)} %get-tuple-element.84.r_5_.r_1_, f32[1024,768]{1,0:T(8,128)} %get-tuple-element.85.r_2_, ...), custom_call_target="tpu_custom_call", output_to_operand_aliasing={{2}: (11, {})} | custom-call | flops 226492416 | bytes 1048576 | tf_op jit(solution)/shard_map/input_grad/pallas_call | solution.py:971
  237.0 2.6 add_convert_fusion.3
  244.4 1.8 slice_dynamic-update-slice_fusion.3
  246.2 3.5 %fusion.23 = (bf16[768,192]{0,1:T(8,128)(2,1)}, f32[768,192]{0,1:T(8,128)}, f32[768,192]{0,1:T(8,128)}, f32[768,192]{0,1:T(8,128)}, f32[192,768]{1,0:T(8,128)}) fusion(f32[768,192]{0,1:T(8,128)S(1)} %copy-done.15, f32[192]{0:T(256)S(1)} %compare_select_fusion, f32[768,192]{0,1:T(8,128)} %param.22, f32[768,192]{0,1:T(8,128)} %param.21, ...), kind=kLoop, calls=%fused_computation.93 | loop fusion | flops 4128768 | bytes 6488832 | tf_op jit(solution)/shard_map/convert_element_type | solution.py:1184
  250.5 2.4 collective-permute-done.40
  252.8 1.8 fusion.11
  255.7 2.4 collective-permute-start.42
  259.2 1.8 slice_dynamic-update-slice_fusion.2
  260.9 3.4 %collective-permute-done.41 = bf16[104,768]{1,0:T(8,128)(2,1)S(1)} collective-permute-done((bf16[104,768]{1,0:T(8,128)(2,1)S(1)}, bf16[104,768]{1,0:T(8,128)(2,1)S(1)}, u32[]{:S(2)}, u32[]{:S(2)}) %collective-permute-start.41) | collective-permute-done | bytes 159776 | tf_op jit(solution)/shard_map/ppermute | solution.py:72
  264.3 6.1 %collective-permute-done.42 = bf16[104,768]{1,0:T(8,128)(2,1)S(1)} collective-permute-done((bf16[104,768]{1,0:T(8,128)(2,1)S(1)}, bf16[104,768]{1,0:T(8,128)(2,1)S(1)}, u32[]{:S(2)}, u32[]{:S(2)}) %collective-permute-start.42) | collective-permute-done | bytes 159776 | tf_op jit(solution)/shard_map/ppermute | solution.py:72
  270.4 1.3 fusion.4
  272.4 1.1 fusion.26
  (215 shorter events, 32.7 us)
Async XLA Ops:
  2.4 17.9 %copy-start.32 = (bf16[104,768]{1,0:T(8,128)(2,1)}, bf16[104,768]{1,0:T(8,128)(2,1)S(1)}, u32[]{:S(2)}) copy-start(bf16[104,768]{1,0:T(8,128)(2,1)S(1)} %fusion.10.r_0_) | copy-start | bytes 479236
  2.4 11.6 %collective-permute-start = (bf16[104,768]{1,0:T(8,128)(2,1)S(1)}, bf16[104,768]{1,0:T(8,128)(2,1)S(1)}, u32[]{:S(2)}, u32[]{:S(2)}) collective-permute-start(bf16[104,768]{1,0:T(8,128)(2,1)S(1)} %fusion.10.r_0_), channel_id=1, source_target_pairs={{0,8},{1,9},{2,10},{3,11},{4,12},{5,13},{6,14},{7,15},{8,0},{9,1},... | collective-permute-start | bytes 479240 | tf_op jit(solution)/shard_map/ppermute | solution.py:72
  5.5 14.8 %collective-permute-start.1 = (bf16[104,768]{1,0:T(8,128)(2,1)S(1)}, bf16[104,768]{1,0:T(8,128)(2,1)S(1)}, u32[]{:S(2)}, u32[]{:S(2)}) collective-permute-start(bf16[104,768]{1,0:T(8,128)(2,1)S(1)} %fusion.10.r_0_), channel_id=1, source_target_pairs={{0,16},{1,17},{2,18},{3,19},{4,20},{5,21},{6,22},{7,23},{8,24},{9,... | collective-permute-start | bytes 479240 | tf_op jit(solution)/shard_map/ppermute | solution.py:72
  8.1 12.2 %collective-permute-start.2 = (bf16[104,768]{1,0:T(8,128)(2,1)S(1)}, bf16[104,768]{1,0:T(8,128)(2,1)S(1)}, u32[]{:S(2)}, u32[]{:S(2)}) collective-permute-start(bf16[104,768]{1,0:T(8,128)(2,1)S(1)} %fusion.10.r_0_), channel_id=1, source_target_pairs={{0,24},{1,25},{2,26},{3,27},{4,28},{5,29},{6,30},{7,31},{8,16},{9,... | collective-permute-start | bytes 479240 | tf_op jit(solution)/shard_map/ppermute | solution.py:72
  9.2 20.8 %collective-permute-start.3 = (bf16[192,768]{1,0:T(8,128)(2,1)S(1)}, bf16[192,768]{1,0:T(8,128)(2,1)S(1)}, u32[]{:S(2)}, u32[]{:S(2)}) collective-permute-start(bf16[192,768]{1,0:T(8,128)(2,1)S(1)} %convert_bitcast_fusion.r_4_.r_0_), channel_id=1, source_target_pairs={{0,8},{1,9},{2,10},{3,11},{4,12},{5,13},{6,14},{7,15},{8,0},{9,1},... | collective-permute-start | bytes 884744 | tf_op jit(solution)/shard_map/ppermute | solution.py:72
  10.1 32.5 %collective-permute-start.4 = (bf16[192,768]{1,0:T(8,128)(2,1)S(1)}, bf16[192,768]{1,0:T(8,128)(2,1)S(1)}, u32[]{:S(2)}, u32[]{:S(2)}) collective-permute-start(bf16[192,768]{1,0:T(8,128)(2,1)S(1)} %convert_bitcast_fusion.r_4_.r_0_), channel_id=1, source_target_pairs={{0,16},{1,17},{2,18},{3,19},{4,20},{5,21},{6,22},{7,23},{8,24},{9,... | collective-permute-start | bytes 884744 | tf_op jit(solution)/shard_map/ppermute | solution.py:72
  14.0 28.7 %collective-permute-start.5 = (bf16[192,768]{1,0:T(8,128)(2,1)S(1)}, bf16[192,768]{1,0:T(8,128)(2,1)S(1)}, u32[]{:S(2)}, u32[]{:S(2)}) collective-permute-start(bf16[192,768]{1,0:T(8,128)(2,1)S(1)} %convert_bitcast_fusion.r_4_.r_0_), channel_id=1, source_target_pairs={{0,24},{1,25},{2,26},{3,27},{4,28},{5,29},{6,30},{7,31},{8,16},{9,... | collective-permute-start | bytes 884744 | tf_op jit(solution)/shard_map/ppermute | solution.py:72
  23.7 16.2 %collective-permute-start.6 = (bf16[4,104,768]{2,1,0:T(8,128)(2,1)}, bf16[4,104,768]{2,1,0:T(8,128)(2,1)S(1)}, u32[]{:S(2)}, u32[]{:S(2)}) collective-permute-start(bf16[4,104,768]{2,1,0:T(8,128)(2,1)} %ordered_stack.2.r_0_), channel_id=1, source_target_pairs={{0,2},{1,5},{2,0},{3,7},{4,6},{5,1},{6,4},{7,3},{8,10},{9,13},{10,... | collective-permute-start | bytes 1916936 | tf_op jit(solution)/shard_map/ppermute | solution.py:72
  25.1 21.3 %collective-permute-start.7 = (bf16[4,104,768]{2,1,0:T(8,128)(2,1)}, bf16[4,104,768]{2,1,0:T(8,128)(2,1)S(1)}, u32[]{:S(2)}, u32[]{:S(2)}) collective-permute-start(bf16[4,104,768]{2,1,0:T(8,128)(2,1)} %ordered_stack.2.r_0_), channel_id=1, source_target_pairs={{0,4},{1,3},{2,6},{3,1},{4,0},{5,7},{6,2},{7,5},{8,12},{9,11},{10,... | collective-permute-start | bytes 1916936 | tf_op jit(solution)/shard_map/ppermute | solution.py:72
  30.0 28.7 %collective-permute-start.13 = (bf16[4,256,768]{2,1,0:T(8,128)(2,1)}, bf16[4,256,768]{2,1,0:T(8,128)(2,1)}, u32[]{:S(2)}, u32[]{:S(2)}) collective-permute-start(bf16[4,256,768]{2,1,0:T(8,128)(2,1)} %r_2_.1), channel_id=1, source_target_pairs={{0,1},{1,0},{2,3},{3,2},{4,5},{5,4},{6,7},{7,6},{8,9},{9,8},{10,11... | collective-permute-start | bytes 4718600 | tf_op jit(solution)/shard_map/ppermute | solution.py:72
  41.5 11.4 %collective-permute-start.8 = (bf16[4,104,768]{2,1,0:T(8,128)(2,1)}, bf16[4,104,768]{2,1,0:T(8,128)(2,1)S(1)}, u32[]{:S(2)}, u32[]{:S(2)}) collective-permute-start(bf16[4,104,768]{2,1,0:T(8,128)(2,1)} %gate.6.r_4_.r_5_.r_8_), channel_id=1, source_target_pairs={{0,4},{1,3},{2,6},{3,1},{4,0},{5,7},{6,2},{7,5},{8,12},{9,11},{10,... | collective-permute-start | bytes 1916936 | tf_op jit(solution)/shard_map/ppermute | solution.py:72
  47.3 6.6 %collective-permute-start.9 = (bf16[4,104,768]{2,1,0:T(8,128)(2,1)}, bf16[4,104,768]{2,1,0:T(8,128)(2,1)S(1)}, u32[]{:S(2)}, u32[]{:S(2)}) collective-permute-start(bf16[4,104,768]{2,1,0:T(8,128)(2,1)} %gate.7.r_4_.r_7_.r_3_), channel_id=1, source_target_pairs={{0,1},{1,0},{2,3},{3,2},{4,5},{5,4},{6,7},{7,6},{8,9},{9,8},{10,11... | collective-permute-start | bytes 1916936 | tf_op jit(solution)/shard_map/ppermute | solution.py:72
  47.8 6.2 %collective-permute-start.10 = (bf16[4,104,768]{2,1,0:T(8,128)(2,1)S(1)}, bf16[4,104,768]{2,1,0:T(8,128)(2,1)S(1)}, u32[]{:S(2)}, u32[]{:S(2)}) collective-permute-start(bf16[4,104,768]{2,1,0:T(8,128)(2,1)S(1)} %copy-done.1), channel_id=1, source_target_pairs={{0,1},{1,0},{2,3},{3,2},{4,5},{5,4},{6,7},{7,6},{8,9},{9,8},{10,11... | collective-permute-start | bytes 1916936 | tf_op jit(solution)/shard_map/ppermute | solution.py:72
  47.8 6.3 %collective-permute-start.11 = (bf16[4,104,768]{2,1,0:T(8,128)(2,1)S(1)}, bf16[4,104,768]{2,1,0:T(8,128)(2,1)S(1)}, u32[]{:S(2)}, u32[]{:S(2)}) collective-permute-start(bf16[4,104,768]{2,1,0:T(8,128)(2,1)S(1)} %collective-permute-done.7.r_6_.r_9_.r_5_), channel_id=1, source_target_pairs={{0,1},{1,0},{2,3},{3,2},{4,5},{5,4},{6,7},{7,6},{8,9},{9,8},{10,11... | collective-permute-start | bytes 1916936 | tf_op jit(solution)/shard_map/ppermute | solution.py:72
  52.8 27.4 %collective-permute-start.14 = (bf16[4,192,768]{2,1,0:T(8,128)(2,1)}, bf16[4,192,768]{2,1,0:T(8,128)(2,1)}, u32[]{:S(2)}, u32[]{:S(2)}) collective-permute-start(bf16[4,192,768]{2,1,0:T(8,128)(2,1)} %ordered_stack.3.r_1_.r_7_), channel_id=1, source_target_pairs={{0,2},{1,5},{2,0},{3,7},{4,6},{5,1},{6,4},{7,3},{8,10},{9,13},{10,... | collective-permute-start | bytes 3538952 | tf_op jit(solution)/shard_map/ppermute | solution.py:72
  53.9 28.9 %collective-permute-start.16 = (bf16[4,192,768]{2,1,0:T(8,128)(2,1)}, bf16[4,192,768]{2,1,0:T(8,128)(2,1)}, u32[]{:S(2)}, u32[]{:S(2)}) collective-permute-start(bf16[4,192,768]{2,1,0:T(8,128)(2,1)} %ordered_stack.3.r_1_.r_7_), channel_id=1, source_target_pairs={{0,4},{1,3},{2,6},{3,1},{4,0},{5,7},{6,2},{7,5},{8,12},{9,11},{10,... | collective-permute-start | bytes 3538952 | tf_op jit(solution)/shard_map/ppermute | solution.py:72
  54.1 2.1 collective-permute-start.12
  80.2 16.5 %collective-permute-start.17 = (bf16[4,192,768]{2,1,0:T(8,128)(2,1)}, bf16[4,192,768]{2,1,0:T(8,128)(2,1)S(1)}, u32[]{:S(2)}, u32[]{:S(2)}) collective-permute-start(bf16[4,192,768]{2,1,0:T(8,128)(2,1)} %gate.8.r_20_.r_8_), channel_id=1, source_target_pairs={{0,4},{1,3},{2,6},{3,1},{4,0},{5,7},{6,2},{7,5},{8,12},{9,11},{10,... | collective-permute-start | bytes 3538952 | tf_op jit(solution)/shard_map/ppermute | solution.py:72
  82.3 15.4 %collective-permute-start.15 = (bf16[4,256,768]{2,1,0:T(8,128)(2,1)S(1)}, bf16[4,256,768]{2,1,0:T(8,128)(2,1)S(1)}, u32[]{:S(2)}, u32[]{:S(2)}) collective-permute-start(bf16[4,256,768]{2,1,0:T(8,128)(2,1)S(1)} %copy-done.16), channel_id=1, source_target_pairs={{0,1},{1,0},{2,3},{3,2},{4,5},{5,4},{6,7},{7,6},{8,9},{9,8},{10,11... | collective-permute-start | bytes 4718600 | tf_op jit(solution)/shard_map/ppermute | solution.py:72
  82.3 15.4 %collective-permute-start.18 = (bf16[4,192,768]{2,1,0:T(8,128)(2,1)}, bf16[4,192,768]{2,1,0:T(8,128)(2,1)S(1)}, u32[]{:S(2)}, u32[]{:S(2)}) collective-permute-start(bf16[4,192,768]{2,1,0:T(8,128)(2,1)} %ordered_stack.3.r_1_.r_7_), channel_id=1, source_target_pairs={{0,1},{1,0},{2,3},{3,2},{4,5},{5,4},{6,7},{7,6},{8,9},{9,8},{10,11... | collective-permute-start | bytes 3538952 | tf_op jit(solution)/shard_map/ppermute | solution.py:72
  82.8 14.9 %collective-permute-start.20 = (bf16[4,192,768]{2,1,0:T(8,128)(2,1)}, bf16[4,192,768]{2,1,0:T(8,128)(2,1)S(1)}, u32[]{:S(2)}, u32[]{:S(2)}) collective-permute-start(bf16[4,192,768]{2,1,0:T(8,128)(2,1)} %collective-permute-done.16.r_9_), channel_id=1, source_target_pairs={{0,1},{1,0},{2,3},{3,2},{4,5},{5,4},{6,7},{7,6},{8,9},{9,8},{10,11... | collective-permute-start | bytes 3538952 | tf_op jit(solution)/shard_map/ppermute | solution.py:72
  82.8 15.0 %collective-permute-start.19 = (bf16[4,192,768]{2,1,0:T(8,128)(2,1)}, bf16[4,192,768]{2,1,0:T(8,128)(2,1)S(1)}, u32[]{:S(2)}, u32[]{:S(2)}) collective-permute-start(bf16[4,192,768]{2,1,0:T(8,128)(2,1)} %gate.8.r_20_.r_8_), channel_id=1, source_target_pairs={{0,1},{1,0},{2,3},{3,2},{4,5},{5,4},{6,7},{7,6},{8,9},{9,8},{10,11... | collective-permute-start | bytes 3538952 | tf_op jit(solution)/shard_map/ppermute | solution.py:72
  97.7 3.1 %collective-permute-start.21 = (bf16[4,192,768]{2,1,0:T(8,128)(2,1)}, bf16[4,192,768]{2,1,0:T(8,128)(2,1)S(1)}, u32[]{:S(2)}, u32[]{:S(2)}) collective-permute-start(bf16[4,192,768]{2,1,0:T(8,128)(2,1)} %gate.9.r_10_), channel_id=1, source_target_pairs={{0,1},{1,0},{2,3},{3,2},{4,5},{5,4},{6,7},{7,6},{8,9},{9,8},{10,11... | collective-permute-start | bytes 3538952 | tf_op jit(solution)/shard_map/ppermute | solution.py:72
  148.9 3.1 %collective-permute-start.23 = (bf16[4,192,768]{2,1,0:T(8,128)(2,1)}, bf16[4,192,768]{2,1,0:T(8,128)(2,1)S(1)}, u32[]{:S(2)}, u32[]{:S(2)}) collective-permute-start(bf16[4,192,768]{2,1,0:T(8,128)(2,1)} %get-tuple-element.74), channel_id=1, source_target_pairs={{0,1},{1,0},{2,3},{3,2},{4,5},{5,4},{6,7},{7,6},{8,9},{9,8},{10,11... | collective-permute-start | bytes 3538952 | tf_op jit(solution)/shard_map/ppermute | solution.py:72
  149.0 6.7 %collective-permute-start.24 = (bf16[4,192,768]{2,1,0:T(8,128)(2,1)}, bf16[4,192,768]{2,1,0:T(8,128)(2,1)S(1)}, u32[]{:S(2)}, u32[]{:S(2)}) collective-permute-start(bf16[4,192,768]{2,1,0:T(8,128)(2,1)} %get-tuple-element.76), channel_id=1, source_target_pairs={{0,1},{1,0},{2,3},{3,2},{4,5},{5,4},{6,7},{7,6},{8,9},{9,8},{10,11... | collective-permute-start | bytes 3538952 | tf_op jit(solution)/shard_map/ppermute | solution.py:72
  149.4 29.1 %collective-permute-start.25 = (bf16[4,192,768]{2,1,0:T(8,128)(2,1)}, bf16[4,192,768]{2,1,0:T(8,128)(2,1)S(1)}, u32[]{:S(2)}, u32[]{:S(2)}) collective-permute-start(bf16[4,192,768]{2,1,0:T(8,128)(2,1)} %get-tuple-element.83), channel_id=1, source_target_pairs={{0,1},{1,0},{2,3},{3,2},{4,5},{5,4},{6,7},{7,6},{8,9},{9,8},{10,11... | collective-permute-start | bytes 3538952 | tf_op jit(solution)/shard_map/ppermute | solution.py:72
  153.7 24.9 %collective-permute-start.26 = (bf16[4,192,768]{2,1,0:T(8,128)(2,1)S(1)}, bf16[4,192,768]{2,1,0:T(8,128)(2,1)S(1)}, u32[]{:S(2)}, u32[]{:S(2)}) collective-permute-start(bf16[4,192,768]{2,1,0:T(8,128)(2,1)S(1)} %add_convert_fusion.2.r_11_.r_7_), channel_id=1, source_target_pairs={{0,4},{1,3},{2,6},{3,1},{4,0},{5,7},{6,2},{7,5},{8,12},{9,11},{10,... | collective-permute-start | bytes 3538952 | tf_op jit(solution)/shard_map/ppermute | solution.py:72
  155.7 34.6 %collective-permute-start.27 = (bf16[4,192,768]{2,1,0:T(8,128)(2,1)}, bf16[4,192,768]{2,1,0:T(8,128)(2,1)S(1)}, u32[]{:S(2)}, u32[]{:S(2)}) collective-permute-start(bf16[4,192,768]{2,1,0:T(8,128)(2,1)} %get-tuple-element.92), channel_id=1, source_target_pairs={{0,1},{1,0},{2,3},{3,2},{4,5},{5,4},{6,7},{7,6},{8,9},{9,8},{10,11... | collective-permute-start | bytes 3538952 | tf_op jit(solution)/shard_map/ppermute | solution.py:72
  156.1 34.3 %collective-permute-start.28 = (bf16[4,192,768]{2,1,0:T(8,128)(2,1)S(1)}, bf16[4,192,768]{2,1,0:T(8,128)(2,1)S(1)}, u32[]{:S(2)}, u32[]{:S(2)}) collective-permute-start(bf16[4,192,768]{2,1,0:T(8,128)(2,1)S(1)} %add_convert_fusion.1.r_12_.r_8_), channel_id=1, source_target_pairs={{0,4},{1,3},{2,6},{3,1},{4,0},{5,7},{6,2},{7,5},{8,12},{9,11},{10,... | collective-permute-start | bytes 3538952 | tf_op jit(solution)/shard_map/ppermute | solution.py:72
  180.3 16.3 %collective-permute-start.29 = (bf16[4,192,768]{2,1,0:T(8,128)(2,1)S(1)}, bf16[4,192,768]{2,1,0:T(8,128)(2,1)S(1)}, u32[]{:S(2)}, u32[]{:S(2)}) collective-permute-start(bf16[4,192,768]{2,1,0:T(8,128)(2,1)S(1)} %add_convert_fusion.r_8_), channel_id=1, source_target_pairs={{0,2},{1,5},{2,0},{3,7},{4,6},{5,1},{6,4},{7,3},{8,10},{9,13},{10,... | collective-permute-start | bytes 3538952 | tf_op jit(solution)/shard_map/ppermute | solution.py:72
  199.4 17.7 %collective-permute-start.30 = (bf16[192,768]{1,0:T(8,128)(2,1)S(1)}, bf16[192,768]{1,0:T(8,128)(2,1)S(1)}, u32[]{:S(2)}, u32[]{:S(2)}) collective-permute-start(bf16[192,768]{1,0:T(8,128)(2,1)S(1)} %get-tuple-element.134.r_9_), channel_id=1, source_target_pairs={{0,16},{1,17},{2,18},{3,19},{4,20},{5,21},{6,22},{7,23},{8,24},{9,... | collective-permute-start | bytes 884744 | tf_op jit(solution)/shard_map/ppermute | solution.py:72
  217.8 2.5 collective-permute-start.31
  217.8 4.3 %collective-permute-start.32 = (bf16[4,104,768]{2,1,0:T(8,128)(2,1)}, bf16[4,104,768]{2,1,0:T(8,128)(2,1)}, u32[]{:S(2)}, u32[]{:S(2)}) collective-permute-start(bf16[4,104,768]{2,1,0:T(8,128)(2,1)} %get-tuple-element.97), channel_id=1, source_target_pairs={{0,1},{1,0},{2,3},{3,2},{4,5},{5,4},{6,7},{7,6},{8,9},{9,8},{10,11... | collective-permute-start | bytes 1916936 | tf_op jit(solution)/shard_map/ppermute | solution.py:72
  218.3 17.6 %collective-permute-start.38 = (bf16[4,104,768]{2,1,0:T(8,128)(2,1)}, bf16[4,104,768]{2,1,0:T(8,128)(2,1)}, u32[]{:S(2)}, u32[]{:S(2)}) collective-permute-start(bf16[4,104,768]{2,1,0:T(8,128)(2,1)} %get-tuple-element.103), channel_id=1, source_target_pairs={{0,1},{1,0},{2,3},{3,2},{4,5},{5,4},{6,7},{7,6},{8,9},{9,8},{10,11... | collective-permute-start | bytes 1916936 | tf_op jit(solution)/shard_map/ppermute | solution.py:72
  220.4 15.6 %collective-permute-start.39 = (bf16[4,104,768]{2,1,0:T(8,128)(2,1)S(1)}, bf16[4,104,768]{2,1,0:T(8,128)(2,1)}, u32[]{:S(2)}, u32[]{:S(2)}) collective-permute-start(bf16[4,104,768]{2,1,0:T(8,128)(2,1)S(1)} %add_convert_fusion.5.r_12_), channel_id=1, source_target_pairs={{0,4},{1,3},{2,6},{3,1},{4,0},{5,7},{6,2},{7,5},{8,12},{9,11},{10,... | collective-permute-start | bytes 1916936 | tf_op jit(solution)/shard_map/ppermute | solution.py:72
  221.5 18.1 %collective-permute-start.22 = (bf16[2,256,768]{2,1,0:T(8,128)(2,1)}, bf16[2,256,768]{2,1,0:T(8,128)(2,1)}, u32[]{:S(2)}, u32[]{:S(2)}) collective-permute-start(bf16[2,256,768]{2,1,0:T(8,128)(2,1)} %get-tuple-element.71), channel_id=1, source_target_pairs={{0,1},{1,0},{2,3},{3,2},{4,5},{5,4},{6,7},{7,6},{8,9},{9,8},{10,11... | collective-permute-start | bytes 2359304 | tf_op jit(solution)/shard_map/ppermute | solution.py:72
  222.1 24.1 %collective-permute-start.34 = (bf16[192,768]{1,0:T(8,128)(2,1)S(1)}, bf16[192,768]{1,0:T(8,128)(2,1)}, u32[]{:S(2)}, u32[]{:S(2)}) collective-permute-start(bf16[192,768]{1,0:T(8,128)(2,1)S(1)} %copy-done.23), channel_id=1, source_target_pairs={{0,8},{1,9},{2,10},{3,11},{4,12},{5,13},{6,14},{7,15},{8,0},{9,1},... | collective-permute-start | bytes 884744 | tf_op jit(solution)/shard_map/ppermute | solution.py:72
  222.1 24.1 %collective-permute-start.35 = (bf16[192,768]{1,0:T(8,128)(2,1)S(1)}, bf16[192,768]{1,0:T(8,128)(2,1)}, u32[]{:S(2)}, u32[]{:S(2)}) collective-permute-start(bf16[192,768]{1,0:T(8,128)(2,1)S(1)} %copy-done.22), channel_id=1, source_target_pairs={{0,24},{1,25},{2,26},{3,27},{4,28},{5,29},{6,30},{7,31},{8,16},{9,... | collective-permute-start | bytes 884744 | tf_op jit(solution)/shard_map/ppermute | solution.py:72
  235.9 13.9 %collective-permute-start.36 = (bf16[4,104,768]{2,1,0:T(8,128)(2,1)}, bf16[4,104,768]{2,1,0:T(8,128)(2,1)}, u32[]{:S(2)}, u32[]{:S(2)}) collective-permute-start(bf16[4,104,768]{2,1,0:T(8,128)(2,1)} %get-tuple-element.101), channel_id=1, source_target_pairs={{0,1},{1,0},{2,3},{3,2},{4,5},{5,4},{6,7},{7,6},{8,9},{9,8},{10,11... | collective-permute-start | bytes 1916936 | tf_op jit(solution)/shard_map/ppermute | solution.py:72
  236.0 14.5 %collective-permute-start.37 = (bf16[4,104,768]{2,1,0:T(8,128)(2,1)S(1)}, bf16[4,104,768]{2,1,0:T(8,128)(2,1)}, u32[]{:S(2)}, u32[]{:S(2)}) collective-permute-start(bf16[4,104,768]{2,1,0:T(8,128)(2,1)S(1)} %copy-done.13), channel_id=1, source_target_pairs={{0,4},{1,3},{2,6},{3,1},{4,0},{5,7},{6,2},{7,5},{8,12},{9,11},{10,... | collective-permute-start | bytes 1916936 | tf_op jit(solution)/shard_map/ppermute | solution.py:72
  239.7 13.2 %collective-permute-start.40 = (bf16[4,104,768]{2,1,0:T(8,128)(2,1)}, bf16[4,104,768]{2,1,0:T(8,128)(2,1)}, u32[]{:S(2)}, u32[]{:S(2)}) collective-permute-start(bf16[4,104,768]{2,1,0:T(8,128)(2,1)} %add_convert_fusion.3), channel_id=1, source_target_pairs={{0,2},{1,5},{2,0},{3,7},{4,6},{5,1},{6,4},{7,3},{8,10},{9,13},{10,... | collective-permute-start | bytes 1916936 | tf_op jit(solution)/shard_map/ppermute | solution.py:72
  246.2 27.3 %collective-permute-start.33 = (f32[2,256,768]{2,1,0:T(8,128)}, f32[2,256,768]{2,1,0:T(8,128)S(1)}, u32[]{:S(2)}, u32[]{:S(2)}) collective-permute-start(f32[2,256,768]{2,1,0:T(8,128)} %get-tuple-element.99), channel_id=1, source_target_pairs={{0,1},{1,0},{2,3},{3,2},{4,5},{5,4},{6,7},{7,6},{8,9},{9,8},{10,11... | collective-permute-start | bytes 4718600 | tf_op jit(solution)/shard_map/ppermute | solution.py:72
  254.7 17.7 %copy-start.25 = (f32[768,96]{0,1:T(8,128)S(1)}, f32[768,96]{0,1:T(8,128)}, u32[]{:S(2)}) copy-start(f32[768,96]{0,1:T(8,128)} %param.17) | copy-start | bytes 884740
  254.7 17.7 %copy-start.35 = (f32[768,96]{0,1:T(8,128)S(1)}, f32[768,96]{0,1:T(8,128)}, u32[]{:S(2)}) copy-start(f32[768,96]{0,1:T(8,128)} %param.19) | copy-start | bytes 884740
  254.7 17.7 %copy-start.36 = (f32[768,96]{0,1:T(8,128)S(1)}, f32[768,96]{0,1:T(8,128)}, u32[]{:S(2)}) copy-start(f32[768,96]{0,1:T(8,128)} %param.18) | copy-start | bytes 884740
  254.7 9.6 %collective-permute-start.41 = (bf16[104,768]{1,0:T(8,128)(2,1)S(1)}, bf16[104,768]{1,0:T(8,128)(2,1)S(1)}, u32[]{:S(2)}, u32[]{:S(2)}) collective-permute-start(bf16[104,768]{1,0:T(8,128)(2,1)S(1)} %get-tuple-element.136), channel_id=1, source_target_pairs={{0,8},{1,9},{2,10},{3,11},{4,12},{5,13},{6,14},{7,15},{8,0},{9,1},... | collective-permute-start | bytes 479240 | tf_op jit(solution)/shard_map/ppermute | solution.py:72
  255.7 14.7 %collective-permute-start.42 = (bf16[104,768]{1,0:T(8,128)(2,1)S(1)}, bf16[104,768]{1,0:T(8,128)(2,1)S(1)}, u32[]{:S(2)}, u32[]{:S(2)}) collective-permute-start(bf16[104,768]{1,0:T(8,128)(2,1)S(1)} %get-tuple-element.138), channel_id=1, source_target_pairs={{0,16},{1,17},{2,18},{3,19},{4,20},{5,21},{6,22},{7,23},{8,24},{9,... | collective-permute-start | bytes 479240 | tf_op jit(solution)/shard_map/ppermute | solution.py:72
  258.1 12.3 %collective-permute-start.43 = (bf16[104,768]{1,0:T(8,128)(2,1)S(1)}, bf16[104,768]{1,0:T(8,128)(2,1)S(1)}, u32[]{:S(2)}, u32[]{:S(2)}) collective-permute-start(bf16[104,768]{1,0:T(8,128)(2,1)S(1)} %get-tuple-element.137), channel_id=1, source_target_pairs={{0,24},{1,25},{2,26},{3,27},{4,28},{5,29},{6,30},{7,31},{8,16},{9,... | collective-permute-start | bytes 479240 | tf_op jit(solution)/shard_map/ppermute | solution.py:72
  (43 other events, 234.3 us)
